TPU v7x, 128 devices: a whole 4x4x4 slice. The times are simulated.
128 devices in a mesh: tower: 4 (over x), dp: 8 (over y_lo, z), mp: 4 (over y_hi, core).
Axes of the slice: x: 4, y: 4 (y_hi: 2, y_lo: 2; y = y_hi * 2 + y_lo), z: 4, core: 2. Of those that a mesh axis runs over, the one named last changes fastest.
Arguments:
- image_in: bfloat16 [4, 1024, 1792], P('tower', 'dp', 'mp'), may hold values from -6 to 6
- text_in: bfloat16 [4, 3072, 1152], P('tower', 'dp', 'mp'), may hold values from -6 to 6
- img_w1: bfloat16 [1792, 7680], P(None, 'mp'), may hold values from -0.125 to 0.125
- img_w2: bfloat16 [7680, 1792], P('mp'), may hold values from -0.0625 to 0.0625
- img_proj: bfloat16 [1792, 1152], P(None, 'mp'), may hold values from -0.125 to 0.125
- txt_w1: bfloat16 [1152, 2560], P(None, 'mp'), may hold values from -0.1875 to 0.1875
- txt_w2: bfloat16 [2560, 1152], P('mp'), may hold values from -0.125 to 0.125
- label_offset: int32 [4, 8], P('tower', 'dp'), may hold values from 0 to 3071
- logit_scale: float32 [], replicated, may hold values from 64 to 72
- logit_bias: float32 [], replicated, may hold values from -10 to -8
- loss_scale: float32 [], replicated, may hold values from 2 to 8
Outputs:
- image_grad: float32 [4, 1024, 1792], P('tower', 'dp', 'mp')
- text_grad: float32 [4, 3072, 1152], P('tower', 'dp', 'mp')
- grad_img_w1: float32 [1792, 7680], P(('tower', 'dp'), 'mp')
- grad_img_w2: float32 [7680, 1792], P('mp', ('tower', 'dp'))
- grad_img_proj: float32 [1792, 1152], P(('tower', 'dp'), 'mp')
- grad_txt_w1: float32 [1152, 2560], P(('tower', 'dp'), 'mp')
- grad_txt_w2: float32 [2560, 1152], P('mp', ('tower', 'dp'))
All inputs are finite; a program needn't handle non-finite values.
Results may differ from a plain program's by a relative error of at most 0.02.
Values may be sent and summed in bfloat16 or wider, within the bound.
A program may use at most 192 MiB of HBM per device.

v0:
```python
import jax
import jax.numpy as jnp
from jax import lax
from jax.sharding import PartitionSpec as P

epsilon = 1e-06


def spread(x, axis, root):
    mine = lax.axis_index(axis) == root
    return lax.psum(jnp.where(mine, x, jnp.zeros_like(x)), axis)


def rms_parts(features):
    widened = features.astype(jnp.float32)
    inverse = lax.rsqrt(jnp.mean(widened * widened, axis=1, keepdims=True) + epsilon)
    return (widened * inverse, inverse)


def contract_rows(first_op, second_op):
    return lax.dot_general(
        first_op, second_op, (((0,), (0,)), ((), ())), preferred_element_type=jnp.float32
    )


def times_transpose(first_op, second_op):
    return lax.dot_general(
        first_op, second_op, (((1,), (1,)), ((), ())), preferred_element_type=jnp.float32
    )


def gelu_grad(preact, upstream):
    _, pullback = jax.vjp(jax.nn.gelu, preact)
    return pullback(upstream)[0]


def input_grad(residual_grad, partial_grad, normed, inverse):
    width = normed.shape[1]
    local_cols = width // lax.axis_size("mp")
    first_col = lax.axis_index("mp") * local_cols
    normed_grad = lax.psum(partial_grad, "mp")
    average = jnp.mean(normed * normed_grad, axis=1, keepdims=True)
    result = residual_grad + (normed_grad - normed * average) * inverse
    return lax.dynamic_slice_in_dim(result, first_col, local_cols, 1)


def layer_front(features, weight_in, weight_out):
    normed, inverse = rms_parts(features)
    preact = jnp.dot(normed.astype(jnp.bfloat16), weight_in, preferred_element_type=jnp.float32)
    hidden = jax.nn.gelu(preact).astype(jnp.bfloat16)
    partial_out = jnp.dot(hidden, weight_out, preferred_element_type=jnp.float32)
    return (inverse, preact, hidden, partial_out)


def blank_front(rows, units, width):
    return (
        jnp.zeros((rows, 1), jnp.float32),
        jnp.zeros((rows, units), jnp.float32),
        jnp.zeros((rows, units), jnp.bfloat16),
        jnp.zeros((rows, width), jnp.float32),
    )


def layer_back(hidden, preact, blended_grad, weight_in, weight_out, normed):
    blended_gb = blended_grad.astype(jnp.bfloat16)
    grad_out = contract_rows(hidden, blended_gb)
    hidden_grad = times_transpose(blended_gb, weight_out)
    preact_grad = gelu_grad(preact, hidden_grad).astype(jnp.bfloat16)
    grad_in = contract_rows(normed.astype(jnp.bfloat16), preact_grad)
    partial_grad = times_transpose(preact_grad, weight_in)
    return (grad_in, grad_out, partial_grad)


def per_device(
    image_in,
    text_in,
    img_w1,
    img_w2,
    img_proj,
    txt_w1,
    txt_w2,
    label_offset,
    logit_scale,
    logit_bias,
    loss_scale,
):
    sections = lax.axis_size("tower")
    mp_count = lax.axis_size("mp")
    text_side = lax.axis_index("tower") == sections - 1
    img_rows = image_in.shape[1]
    img_width = image_in.shape[2] * mp_count
    txt_rows = text_in.shape[1]
    txt_width = text_in.shape[2] * mp_count
    share_rows = txt_rows // mp_count
    img_units = img_w1.shape[1]
    txt_units = txt_w1.shape[1]
    column_count = share_rows * lax.axis_size("dp")
    img_feat = lax.all_gather(image_in[0], "mp", axis=1, tiled=True)
    txt_feat = lax.all_gather(text_in[0], "mp", axis=1, tiled=True)

    def front_image(operand):
        return layer_front(img_feat, img_w1, img_w2) + blank_front(txt_rows, txt_units, txt_width)

    def front_text(operand):
        return blank_front(img_rows, img_units, img_width) + layer_front(txt_feat, txt_w1, txt_w2)

    (
        img_inverse,
        img_preact,
        img_hidden,
        img_partial,
        txt_inverse,
        txt_preact,
        txt_hidden,
        txt_partial,
    ) = lax.cond(text_side, front_text, front_image, 0)
    img_blended = img_feat.astype(jnp.float32) + lax.psum(img_partial, "mp")
    txt_blended = txt_feat.astype(jnp.float32) + lax.psum(txt_partial, "mp")
    blended_b = img_blended.astype(jnp.bfloat16)
    head_local = jnp.dot(blended_b, img_proj, preferred_element_type=jnp.float32)
    projected = lax.all_gather(head_local, "mp", axis=1, tiled=True)
    length = jnp.sqrt(jnp.sum(projected * projected, axis=1, keepdims=True))
    embedded = (projected / length).astype(jnp.bfloat16)
    txt_length = jnp.sqrt(jnp.sum(txt_blended * txt_blended, axis=1, keepdims=True))
    txt_embed = (txt_blended / txt_length).astype(jnp.bfloat16)
    text_piece = lax.dynamic_slice_in_dim(
        txt_embed, lax.axis_index("mp") * share_rows, share_rows, 0
    )
    reached = spread(text_piece, "tower", sections - 1)
    columns = lax.all_gather(reached, "dp", axis=0, tiled=True)

    def loss_image(operand):
        scores = times_transpose(embedded, columns)
        logits = logit_scale * scores + logit_bias
        first_row = (
            lax.axis_index("tower") * lax.axis_size("dp") + lax.axis_index("dp")
        ) * img_rows
        row_ids = first_row + jnp.arange(img_rows, dtype=jnp.int32)
        target = (row_ids + label_offset[0, 0]) % (txt_rows * lax.axis_size("dp"))
        owning = target % txt_rows // share_rows
        position = target // txt_rows * share_rows + target % share_rows
        col_ids = jnp.arange(column_count, dtype=jnp.int32)
        positive = (owning == lax.axis_index("mp"))[:, None] & (
            col_ids[None, :] == position[:, None]
        )
        signed = jnp.where(positive, jnp.float32(1.0), jnp.float32(-1.0))
        pair_grad = -loss_scale * signed * jax.nn.sigmoid(-signed * logits)
        pair_weight = (logit_scale * pair_grad).astype(jnp.bfloat16)
        partial_embed = jnp.dot(pair_weight, columns, preferred_element_type=jnp.float32)
        return (partial_embed, pair_weight)

    def loss_text(operand):
        return (
            jnp.zeros((img_rows, txt_width), jnp.float32),
            jnp.zeros((img_rows, column_count), jnp.bfloat16),
        )

    partial_embed, pair_weight = lax.cond(text_side, loss_text, loss_image, 0)
    embed_grad = lax.psum(partial_embed, "mp")
    section_grad = lax.psum_scatter(
        contract_rows(pair_weight, embedded), "dp", scatter_dimension=0, tiled=True
    )
    text_grad_share = lax.psum(section_grad, "tower")
    full_grad = lax.all_gather(text_grad_share, "mp", axis=0, tiled=True)
    direction = projected / length
    proj_full = (
        embed_grad - direction * jnp.sum(direction * embed_grad, axis=1, keepdims=True)
    ) / length
    local_cols = img_proj.shape[1]
    proj_grad = lax.dynamic_slice_in_dim(
        proj_full, lax.axis_index("mp") * local_cols, local_cols, 1
    ).astype(jnp.bfloat16)
    proj_grad = jnp.where(text_side, jnp.zeros_like(proj_grad), proj_grad)
    grad_proj = contract_rows(blended_b, proj_grad)
    img_bgrad = lax.psum(times_transpose(proj_grad, img_proj), "mp")
    txt_direction = txt_blended / txt_length
    txt_bgrad = (
        full_grad - txt_direction * jnp.sum(txt_direction * full_grad, axis=1, keepdims=True)
    ) / txt_length
    txt_bgrad = jnp.where(text_side, txt_bgrad, jnp.zeros_like(txt_bgrad))
    img_normed = img_feat.astype(jnp.float32) * img_inverse
    txt_normed = txt_feat.astype(jnp.float32) * txt_inverse

    def back_image(operand):
        grad_in, grad_out, partial_grad = layer_back(
            img_hidden, img_preact, img_bgrad, img_w1, img_w2, img_normed
        )
        return (
            grad_in,
            grad_out,
            partial_grad,
            jnp.zeros(txt_w1.shape, jnp.float32),
            jnp.zeros(txt_w2.shape, jnp.float32),
            jnp.zeros((txt_rows, txt_width), jnp.float32),
        )

    def back_text(operand):
        grad_in, grad_out, partial_grad = layer_back(
            txt_hidden, txt_preact, txt_bgrad, txt_w1, txt_w2, txt_normed
        )
        return (
            jnp.zeros(img_w1.shape, jnp.float32),
            jnp.zeros(img_w2.shape, jnp.float32),
            jnp.zeros((img_rows, img_width), jnp.float32),
            grad_in,
            grad_out,
            partial_grad,
        )

    grad_w1, grad_w2, img_part, grad_t1, grad_t2, txt_part = lax.cond(
        text_side, back_text, back_image, 0
    )
    image_dx = input_grad(img_bgrad, img_part, img_normed, img_inverse)
    text_dx = input_grad(txt_bgrad, txt_part, txt_normed, txt_inverse)
    row_sums = (
        lax.psum_scatter(
            grad_w1.astype(jnp.bfloat16), ("tower", "dp"), scatter_dimension=0, tiled=True
        ).astype(jnp.float32),
        lax.psum_scatter(
            grad_proj.astype(jnp.bfloat16), ("tower", "dp"), scatter_dimension=0, tiled=True
        ).astype(jnp.float32),
        lax.psum_scatter(
            grad_t1.astype(jnp.bfloat16), ("tower", "dp"), scatter_dimension=0, tiled=True
        ).astype(jnp.float32),
    )
    col_sums = (
        lax.psum_scatter(
            grad_w2.astype(jnp.bfloat16), ("tower", "dp"), scatter_dimension=1, tiled=True
        ).astype(jnp.float32),
        lax.psum_scatter(
            grad_t2.astype(jnp.bfloat16), ("tower", "dp"), scatter_dimension=1, tiled=True
        ).astype(jnp.float32),
    )
    return (
        image_dx[None],
        text_dx[None],
        row_sums[0],
        col_sums[0],
        row_sums[1],
        row_sums[2],
        col_sums[1],
    )


def solution(mesh):
    return jax.shard_map(
        per_device,
        mesh=mesh,
        in_specs=(
            P("tower", "dp", "mp"),
            P("tower", "dp", "mp"),
            P(None, "mp"),
            P("mp", None),
            P(None, "mp"),
            P(None, "mp"),
            P("mp", None),
            P("tower", "dp"),
            P(),
            P(),
            P(),
        ),
        out_specs=(
            P("tower", "dp", "mp"),
            P("tower", "dp", "mp"),
            P(("tower", "dp"), "mp"),
            P("mp", ("tower", "dp")),
            P(("tower", "dp"), "mp"),
            P(("tower", "dp"), "mp"),
            P("mp", ("tower", "dp")),
        ),
        check_vma=False,
    )
```

profile of v0, /device:TPU:0, one launch (start us, length us, event | category | flops | bytes accessed | tf_op | source)
XLA Modules:
  0.0 1028.3 jit_solution(13674277875548996950)
XLA Ops:
  7.2 8.9 all-gather
  16.4 11.0 %all-gather.1 = bf16[1,384,1152]{1,2,0:T(8,128)(2,1)S(1)} all-gather(bf16[1,384,288]{1,2,0:T(8,128)(2,1)} %param.18), channel_id=3, replica_groups=mesh['tower'=4,'dp'=8,'mp'=4] {'mp'}, dimensions={2}, use_global_device_ids=true | all-gather | bytes 1105920 | tf_op jit(solution)/shard_map/all_gather | solution.py:99
  28.2 10.9 %conditional.3 = (f32[128,1]{0,1:T(1,128)}, f32[128,1920]{1,0:T(8,128)}, bf16[128,1920]{1,0:T(8,128)(2,1)S(1)}, f32[128,1792]{1,0:T(8,128)}, f32[384,1]{1,0:T(8,...) conditional(s32[]{:T(128)} %convert_element_type.94, ...), branch_computations={%region_0.0_spmd, %region_2.0_spmd} | conditional | flops 1765195904 | bytes 41455740 | solution.py:116
  29.0 5.6 fusion.9
  39.9 69.8 %all-reduce.27.cloned.1.call-done = (f32[128,1792]{1,0:T(8,128)}, f32[384,1152]{1,0:T(8,128)}) async-done(((f32[128,1792]{1,0:T(8,128)}, f32[384,1152]{1,0:T(8,128)}), (f32[128,1792]{1,0:T(8,128)}, f32[384,1152]{1,0:T(8,128)})) %all-reduce.27.cloned.1.call-update) | async-done | bytes 2686992 | tf_op jit(solution)/shard_map/psum | solution.py:117
  115.6 41.0 %all-reduce.17.cloned.1.call-done = bf16[96,1152]{1,0:T(8,128)(2,1)} async-done(((bf16[96,1152]{1,0:T(8,128)(2,1)}), bf16[96,1152]{1,0:T(8,128)(2,1)}) %all-reduce.17.cloned.1.call-update) | async-done | bytes 221200 | tf_op jit(solution)/shard_map/psum | solution.py:11
  158.4 9.0 all_gather.17
  169.1 30.7 %all-gather.5.cloned.1.call-done = bf16[768,1152]{1,0:T(8,128)(2,1)} async-done(((bf16[96,1152]{1,0:T(8,128)(2,1)}), bf16[768,1152]{1,0:T(8,128)(2,1)}) %all-gather.5.cloned.1.call-update) | async-done | bytes 1769488 | tf_op jit(solution)/shard_map/all_gather | solution.py:130
  199.8 7.0 conditional.4
  212.5 45.6 %reduce-scatter.18.cloned.1.call-done = f32[96,1152]{1,0:T(8,128)} async-done(((f32[768,1152]{1,0:T(8,128)}), f32[96,1152]{1,0:T(8,128)}) %reduce-scatter.18.cloned.1.call-update) | async-done | bytes 442384 | tf_op jit(solution)/shard_map/reduce_scatter | solution.py:160
  258.2 43.9 %all-reduce.19.cloned.1.call-done = f32[128,1152]{0,1:T(8,128)} async-done(((f32[128,1152]{0,1:T(8,128)}), f32[128,1152]{0,1:T(8,128)}) %all-reduce.19.cloned.1.call-update) | async-done | bytes 589840 | tf_op jit(solution)/shard_map/psum | solution.py:159
  306.0 40.4 %all-reduce.23.cloned.1.call-done = f32[96,1152]{1,0:T(8,128)} async-done(((f32[96,1152]{1,0:T(8,128)}), f32[96,1152]{1,0:T(8,128)}) %all-reduce.23.cloned.1.call-update) | async-done | bytes 442384 | tf_op jit(solution)/shard_map/psum | solution.py:163
  350.1 43.8 %all-reduce.21.cloned.1.call-done = f32[128,1792]{1,0:T(8,128)} async-done(((f32[128,1792]{1,0:T(8,128)}), f32[128,1792]{1,0:T(8,128)}) %all-reduce.21.cloned.1.call-update) | async-done | bytes 917520 | tf_op jit(solution)/shard_map/psum | solution.py:175
  393.8 26.2 %all-gather.7.cloned.1.call-done = f32[384,1152]{1,0:T(8,128)} async-done(((f32[96,1152]{1,0:T(8,128)}), f32[384,1152]{1,0:T(8,128)}) %all-gather.7.cloned.1.call-update) | async-done | bytes 1769488 | tf_op jit(solution)/shard_map/all_gather | solution.py:164
  425.9 22.1 %conditional.5 = (bf16[1792,1920]{0,1:T(8,128)(2,1)}, bf16[1920,1792]{1,0:T(8,128)(2,1)}, f32[128,1792]{1,0:T(8,128)}, bf16[1152,640]{1,0:T(8,128)(2,1)}, bf16[6...) conditional(s32[]{:T(128)} %convert_element_type.94, (f32[128,1792]{1,0:T(8,128)S(1)}, bf16[1920,1792]{1,0:T(8,128)(2,1)}, ...), branch_computations={%region_17.18_spmd, %region_18.19_spmd} | conditional | flops 3528818688 | bytes 66388056 | solution.py:210
  425.9 5.7 fusion.47
  448.1 9.9 copy.60
  458.1 9.9 copy.61
  471.6 100.4 %fusion.80 = (bf16[48,640]{1,0:T(8,128)(2,1)S(1)}, bf16[640,48]{0,1:T(8,128)(2,1)S(1)}) fusion(bf16[1152,640]{1,0:T(8,128)(2,1)} %get-tuple-element.109, bf16[640,1152]{0,1:T(8,128)(2,1)} %copy.62), kind=kCustom, calls=%all-reduce-scatter.2 | all-reduce-scatter fusion | flops 1966081 | bytes 3072512
  597.4 7.9 collective-permute-start.14
  627.6 6.7 concatenate.1
  635.6 23.5 %all-reduce.25.cloned.1.call-done = (f32[128,1792]{1,0:T(8,128)}, f32[384,1152]{1,0:T(8,128)}) async-done(((f32[128,1792]{1,0:T(8,128)}, f32[384,1152]{1,0:T(8,128)}), (f32[128,1792]{1,0:T(8,128)}, f32[384,1152]{1,0:T(8,128)})) %all-reduce.25.cloned.1.call-update) | async-done | bytes 2686992 | tf_op jit(solution)/shard_map/psum | solution.py:41
  668.0 172.8 %reduce-scatter.20.cloned.1.call-done = bf16[56,1920]{1,0:T(8,128)(2,1)} async-done(((bf16[1792,1920]{1,0:T(8,128)(2,1)}), bf16[56,1920]{1,0:T(8,128)(2,1)}) %reduce-scatter.20.cloned.1.call-update) | async-done | bytes 215056
  842.4 177.3 %reduce-scatter.22.cloned.1.call-done = bf16[1920,56]{0,1:T(8,128)(2,1)} async-done(((bf16[1920,1792]{0,1:T(8,128)(2,1)}), bf16[1920,56]{0,1:T(8,128)(2,1)}) %reduce-scatter.22.cloned.1.call-update) | async-done | bytes 215056
  (159 shorter events, 122.4 us)
Async XLA Ops:
  7.2 102.6 %all-reduce.27.cloned.1.call-start = ((), (), s32[]{:S(2)}) async-start(), calls=%async_computation.15 | async-start | bytes 5373952 | tf_op jit(solution)/shard_map/psum | solution.py:117
  39.2 117.5 %all-reduce.17.cloned.1.call-start = ((), (), s32[]{:S(2)}) async-start(), calls=%async_computation.4 | async-start | bytes 442368 | tf_op jit(solution)/shard_map/psum | solution.py:11
  115.6 84.2 %all-gather.5.cloned.1.call-start = ((), (), s32[]{:S(2)}) async-start(), calls=%async_computation.5 | async-start | bytes 1990656 | tf_op jit(solution)/shard_map/all_gather | solution.py:130
  156.7 101.4 %reduce-scatter.18.cloned.1.call-start = ((), (), s32[]{:S(2)}) async-start(), calls=%async_computation.8 | async-start | bytes 3981312 | tf_op jit(solution)/shard_map/reduce_scatter | solution.py:160
  210.2 91.9 %all-reduce.19.cloned.1.call-start = ((), (), s32[]{:S(2)}) async-start(), calls=%async_computation.6 | async-start | bytes 1179648 | tf_op jit(solution)/shard_map/psum | solution.py:159
  212.5 133.9 %all-reduce.23.cloned.1.call-start = ((), (), s32[]{:S(2)}) async-start(), calls=%async_computation.9 | async-start | bytes 884736 | tf_op jit(solution)/shard_map/psum | solution.py:163
  258.1 135.7 %all-reduce.21.cloned.1.call-start = ((), (), s32[]{:S(2)}) async-start(), calls=%async_computation.7 | async-start | bytes 1835008 | tf_op jit(solution)/shard_map/psum | solution.py:175
  305.9 114.1 %all-gather.7.cloned.1.call-start = ((), (), s32[]{:S(2)}) async-start(), calls=%async_computation.10 | async-start | bytes 2211840 | tf_op jit(solution)/shard_map/all_gather | solution.py:164
  346.3 277.1 %reduce-scatter.24.cloned.1.call-start = ((), (), s32[]{:S(2)}) async-start(), calls=%async_computation.13 | async-start | bytes 1419264
  349.0 310.1 %all-reduce.25.cloned.1.call-start = ((), (), s32[]{:S(2)}) async-start(), calls=%async_computation.14 | async-start | bytes 5373952 | tf_op jit(solution)/shard_map/psum | solution.py:41
  448.0 392.7 %reduce-scatter.20.cloned.1.call-start = ((), (), s32[]{:S(2)}) async-start(), calls=%async_computation.11 | async-start | bytes 7096320
  458.0 561.7 %reduce-scatter.22.cloned.1.call-start = ((), (), s32[]{:S(2)}) async-start(), calls=%async_computation.12 | async-start | bytes 7096320
  573.3 18.3 %collective-permute-start.6 = (bf16[48,640]{1,0:T(8,128)(2,1)S(1)}, bf16[48,640]{1,0:T(8,128)(2,1)S(1)}, u32[]{:S(2)}, u32[]{:S(2)}) collective-permute-start(bf16[48,640]{1,0:T(8,128)(2,1)S(1)} %get-tuple-element.197), channel_id=1, source_target_pairs={{0,28},{4,32},{8,36},{12,40},{16,44},{20,48},{24,52},{28,56},{32,6... | collective-permute-start | bytes 184328
  574.6 20.9 %collective-permute-start.5 = (bf16[48,640]{1,0:T(8,128)(2,1)S(1)}, bf16[48,640]{1,0:T(8,128)(2,1)S(1)}, u32[]{:S(2)}, u32[]{:S(2)}) collective-permute-start(bf16[48,640]{1,0:T(8,128)(2,1)S(1)} %get-tuple-element.197), channel_id=1, source_target_pairs={{0,24},{4,28},{8,32},{12,36},{16,40},{20,44},{24,48},{28,52},{32,5... | collective-permute-start | bytes 184328
  575.9 21.5 %collective-permute-start.4 = (bf16[48,640]{1,0:T(8,128)(2,1)S(1)}, bf16[48,640]{1,0:T(8,128)(2,1)S(1)}, u32[]{:S(2)}, u32[]{:S(2)}) collective-permute-start(bf16[48,640]{1,0:T(8,128)(2,1)S(1)} %get-tuple-element.197), channel_id=1, source_target_pairs={{0,20},{4,24},{8,28},{12,32},{16,36},{20,40},{24,44},{28,48},{32,5... | collective-permute-start | bytes 184328
  577.2 28.1 %collective-permute-start.3 = (bf16[48,640]{1,0:T(8,128)(2,1)S(1)}, bf16[48,640]{1,0:T(8,128)(2,1)S(1)}, u32[]{:S(2)}, u32[]{:S(2)}) collective-permute-start(bf16[48,640]{1,0:T(8,128)(2,1)S(1)} %get-tuple-element.197), channel_id=1, source_target_pairs={{0,16},{4,20},{8,24},{12,28},{16,32},{20,36},{24,40},{28,44},{32,4... | collective-permute-start | bytes 184328
  588.8 18.2 %collective-permute-start.2 = (bf16[48,640]{1,0:T(8,128)(2,1)S(1)}, bf16[48,640]{1,0:T(8,128)(2,1)S(1)}, u32[]{:S(2)}, u32[]{:S(2)}) collective-permute-start(bf16[48,640]{1,0:T(8,128)(2,1)S(1)} %get-tuple-element.197), channel_id=1, source_target_pairs={{0,12},{4,16},{8,20},{12,24},{16,28},{20,32},{24,36},{28,40},{32,4... | collective-permute-start | bytes 184328
  591.6 19.9 %collective-permute-start.1 = (bf16[48,640]{1,0:T(8,128)(2,1)S(1)}, bf16[48,640]{1,0:T(8,128)(2,1)S(1)}, u32[]{:S(2)}, u32[]{:S(2)}) collective-permute-start(bf16[48,640]{1,0:T(8,128)(2,1)S(1)} %get-tuple-element.197), channel_id=1, source_target_pairs={{0,8},{4,12},{8,16},{12,20},{16,24},{20,28},{24,32},{28,36},{32,40... | collective-permute-start | bytes 184328
  595.6 18.5 %collective-permute-start = (bf16[48,640]{1,0:T(8,128)(2,1)S(1)}, bf16[48,640]{1,0:T(8,128)(2,1)S(1)}, u32[]{:S(2)}, u32[]{:S(2)}) collective-permute-start(bf16[48,640]{1,0:T(8,128)(2,1)S(1)} %get-tuple-element.197), channel_id=1, source_target_pairs={{0,4},{4,8},{8,12},{12,16},{16,20},{20,24},{24,28},{28,32},{32,36}... | collective-permute-start | bytes 184328
  597.4 19.5 %collective-permute-start.14 = (bf16[640,48]{0,1:T(8,128)(2,1)S(1)}, bf16[640,48]{0,1:T(8,128)(2,1)S(1)}, u32[]{:S(2)}, u32[]{:S(2)}) collective-permute-start(bf16[640,48]{0,1:T(8,128)(2,1)S(1)} %get-tuple-element.198), channel_id=1, source_target_pairs={{0,28},{4,32},{8,36},{12,40},{16,44},{20,48},{24,52},{28,56},{32,6... | collective-permute-start | bytes 184328
  605.3 14.7 %collective-permute-start.13 = (bf16[640,48]{0,1:T(8,128)(2,1)S(1)}, bf16[640,48]{0,1:T(8,128)(2,1)S(1)}, u32[]{:S(2)}, u32[]{:S(2)}) collective-permute-start(bf16[640,48]{0,1:T(8,128)(2,1)S(1)} %get-tuple-element.198), channel_id=1, source_target_pairs={{0,24},{4,28},{8,32},{12,36},{16,40},{20,44},{24,48},{28,52},{32,5... | collective-permute-start | bytes 184328
  607.0 20.6 %collective-permute-start.12 = (bf16[640,48]{0,1:T(8,128)(2,1)S(1)}, bf16[640,48]{0,1:T(8,128)(2,1)}, u32[]{:S(2)}, u32[]{:S(2)}) collective-permute-start(bf16[640,48]{0,1:T(8,128)(2,1)S(1)} %get-tuple-element.198), channel_id=1, source_target_pairs={{0,20},{4,24},{8,28},{12,32},{16,36},{20,40},{24,44},{28,48},{32,5... | collective-permute-start | bytes 184328
  611.5 16.0 %collective-permute-start.11 = (bf16[640,48]{0,1:T(8,128)(2,1)S(1)}, bf16[640,48]{0,1:T(8,128)(2,1)}, u32[]{:S(2)}, u32[]{:S(2)}) collective-permute-start(bf16[640,48]{0,1:T(8,128)(2,1)S(1)} %get-tuple-element.198), channel_id=1, source_target_pairs={{0,16},{4,20},{8,24},{12,28},{16,32},{20,36},{24,40},{28,44},{32,4... | collective-permute-start | bytes 184328
  614.1 13.5 %collective-permute-start.10 = (bf16[640,48]{0,1:T(8,128)(2,1)S(1)}, bf16[640,48]{0,1:T(8,128)(2,1)}, u32[]{:S(2)}, u32[]{:S(2)}) collective-permute-start(bf16[640,48]{0,1:T(8,128)(2,1)S(1)} %get-tuple-element.198), channel_id=1, source_target_pairs={{0,12},{4,16},{8,20},{12,24},{16,28},{20,32},{24,36},{28,40},{32,4... | collective-permute-start | bytes 184328
  (28 other events, 978.7 us)
Sparse Core Ops, SparseCore 0:
  39.3 70.4 all-reduce.26
  115.7 40.9 all-reduce.16
  158.3 41.4 all-gather.4
  210.3 47.7 reduce-scatter.17
  260.6 41.4 all-reduce.18
  304.4 41.8 all-reduce.22
  348.8 44.9 all-reduce.20
  395.5 24.4 all-gather.6
  422.4 163.0 reduce-scatter.23
  588.1 70.9 all-reduce.24
  661.5 179.1 reduce-scatter.19
  843.1 176.5 reduce-scatter.21
where the time goes:
time: 1030 us
  waiting for transfers between devices  717 us (70%)
  blocking collectives  129 us (13%)
  local copies, waits for them, and re-layouts  49.9 us (5%)
  starting transfers between devices  48.9 us (5%)
  matrix products  41 us (4%)
  other arithmetic  26.2 us (3%)
  between operations  15.3 us (1%)
    unnamed x31, waiting for transfers between devices  352 us
    unnamed x1, blocking collectives  100 us
    psum x1, waiting for transfers between devices, per_device(): img_blended = img_feat.astype(jnp.float32) + lax.psum(img_partial, 'mp')  69.8 us
    unnamed x19, starting transfers between devices  48.3 us
    reduce_scatter x1, waiting for transfers between devices, per_device(): lax.psum_scatter(contract_rows(pair_weight, embedded), 'dp', scatter_dime...  45.6 us
    psum x1, waiting for transfers between devices, per_device(): embed_grad = lax.psum(partial_embed, 'mp')  43.9 us
    psum x1, waiting for transfers between devices, per_device(): img_bgrad = lax.psum(times_transpose(proj_grad, img_proj), 'mp')  43.8 us
    psum x1, waiting for transfers between devices, spread(): return lax.psum(jnp.where(mine, x, jnp.zeros_like(x)), axis)  41 us
  transfers between devices with their start and end apart: 28, of which 12 were waited for; matrix products, arithmetic and copies ran while one was open for 18% of the time, Pallas kernels for 0%

commit v1 on v0

v1 whole, which is shorter than its diff:
```python
import functools
import math

import jax
import jax.numpy as jnp
from jax import lax
from jax.experimental import pallas as pl
from jax.experimental.pallas import tpu as pltpu
from jax.sharding import PartitionSpec as P

epsilon = 1e-06
bf16 = jnp.bfloat16
f32 = jnp.float32
MESH = pl.DeviceIdType.MESH
GELU_A = math.sqrt(2.0 / math.pi)
GELU_B = 0.044715

NT = 4
ND = 8
NM = 4
IR = 128
TR = 384
IQ = IR // NM
TQ = TR // NM
WI = 1792
WT = 1152
IS = WI // NM
TS = WT // NM
FI = 1920
FT = 640
BATCH = 3072
IO = WI // 32
TO = WT // 32
IP = 64
TP = 48
N_SEM = 320


def dot(a, b):
    return jnp.dot(a, b, preferred_element_type=f32)


def dot_t(a, b):
    return lax.dot_general(a, b, (((1,), (1,)), ((), ())), preferred_element_type=f32)


def dot_rows(a, b):
    return lax.dot_general(a, b, (((0,), (0,)), ((), ())), preferred_element_type=f32)


def gelu_both(u):
    sq = u * u
    th = jnp.tanh(GELU_A * u * (1.0 + GELU_B * sq))
    half = 0.5 * (1.0 + th)
    slope = half + 0.5 * u * (1.0 - th * th) * (GELU_A * (1.0 + 3.0 * GELU_B * sq))
    return u * half, slope


def scratch_list():
    v = pltpu.VMEM
    return dict(
        w1=v((WI, FI), bf16),
        w2=v((FI, WI), bf16),
        pj=v((NM, WI, TS), bf16),
        xs=v((NM, IR, IS), bf16),
        xt=v((NM, TR, TS), bf16),
        ns=v((NM, IR, IS), bf16),
        nt=v((NM, TR, TS), bf16),
        ivi=v((IR, 1), f32),
        ivt=v((TR, 1), f32),
        hi=v((3, IR, FI), bf16),
        ht=v((TR, FT), bf16),
        gi=v((IR, FI), f32),
        gt=v((TR, FT), f32),
        p2i=v((IR, WI), f32),
        p2t=v((TR, WT), f32),
        rc2i=v((2, IQ, WI), f32),
        rc2t=v((2, TQ, WT), f32),
        st2i=v((IQ, WI), bf16),
        st2t=v((TQ, WT), bf16),
        rx2i=v((IQ, WI), bf16),
        rx2t=v((TQ, WT), bf16),
        tb=v((TQ, WT), f32),
        tl=v((TQ, 1), f32),
        bl=v((NM, NM, IQ, IS), bf16),
        pr=v((IQ, WT), f32),
        ln=v((IQ, 1), f32),
        ei=v((NM, IQ, WT), bf16),
        et=v((NM, TQ, WT), bf16),
        cols=v((ND, TQ, WT), bf16),
        lab=v((ND, 3, 8, 128), f32),
        labo=v((8, 128), f32),
        q4t=v((TR, WT), f32),
        rc4t=v((2, TQ, WT), f32),
        st4t=v((TQ, WT), bf16),
        rx4t=v((TQ, WT), bf16),
        bfi=v((NM, IQ, WI), bf16),
        bft=v((NM, TQ, WT), bf16),
        pgs=v((NM, IQ, TS), bf16),
        pgr=v((NM, IQ, TS), bf16),
        bsi=v((NM, IR, IS), bf16),
        bst=v((NM, TR, TS), bf16),
        an=v((3, IR, IS), bf16),
        ant=v((TR, TS), bf16),
        ab=v((3, IR, IS), bf16),
        abt=v((TR, TS), bf16),
        al=v((3, NM, IQ, IS), bf16),
        bj=v((3, NM, IQ, TS), bf16),
        ki=v((3, IR, FI), bf16),
        kt=v((TR, FT), bf16),
        g6i=v((NM, IR, 512), f32),
        g6t=v((NM, TR, 384), f32),
        rc6i=v((2, IR, 512), f32),
        rc6t=v((2, TR, 384), f32),
        st6i=v((IR, 512), bf16),
        st6t=v((TR, 384), bf16),
        rx6i=v((IR, 512), bf16),
        rx6t=v((TR, 384), bf16),
        rb1=v((ND, IP, FI), bf16),
        sb2=v((ND, IP, FI), bf16),
        rb2=v((ND, IP, FI), bf16),
        sbj=v((ND, IP, TS), bf16),
        rbj=v((ND, IP, TS), bf16),
        sbt1=v((ND, TP, FT), bf16),
        rbt1=v((ND, TP, FT), bf16),
        sbt2=v((ND, TP, FT), bf16),
        rbt2=v((ND, TP, FT), bf16),
        sem=pltpu.SemaphoreType.DMA((N_SEM,)),
    )


NAMES = list(scratch_list())


def step_kernel(
    img_in, txt_in, w1_in, w2_in, pj_in, tw1_in, tw2_in, label, scale, bias, loss,
    o_img, o_txt, o_w1, o_w2, o_pj, o_t1, o_t2, *scratch
):
    r = dict(zip(NAMES, scratch))
    sem = r["sem"]
    used = [0]
    t = lax.axis_index("tower")
    d = lax.axis_index("dp")
    m = lax.axis_index("mp")
    core = m % 2
    high = m // 2
    ms = m + 1 - 2 * core
    mo = (m + 2) % NM
    md = (ms + 2) % NM
    text = t == NT - 1
    image = t != NT - 1
    ti = jnp.minimum(t, 2)
    sib, opp, diag = (t, d, ms), (t, d, mo), (t, d, md)
    others_t = [((t + k) % NT, d, m) for k in (1, 2, 3)]
    order_d = (4, 1, 3, 5, 7, 2, 6)
    others_d = [(d + k) % ND for k in order_d]

    def take(n):
        first = used[0]
        used[0] += n
        assert used[0] <= N_SEM
        return first

    img_sends, txt_sends, all_sends = [], [], []

    def send(src, dst, arrived, dev, group):
        copy = pltpu.make_async_remote_copy(
            src_ref=src, dst_ref=dst, send_sem=sem.at[take(1)], recv_sem=sem.at[arrived],
            device_id=dev, device_id_type=MESH,
        )
        group.append(copy)
        return copy

    def arrive(dst, arrived):
        pltpu.make_async_remote_copy(
            src_ref=dst, dst_ref=dst, send_sem=sem.at[0], recv_sem=sem.at[arrived],
            device_id=sib, device_id_type=MESH,
        ).wait_recv()

    def gather_mp(slot, group):
        b = take(NM)
        to_opp = send(slot(m), slot(m), b + m, opp, group)
        to_sib = send(slot(m), slot(m), b + m, sib, group)
        pass_on = send(slot(mo), slot(mo), b + mo, sib, group)

        def start():
            to_opp.start()
            to_sib.start()

        def middle():
            arrive(slot(mo), b + mo)
            pass_on.start()

        def finish():
            arrive(slot(ms), b + ms)
            arrive(slot(md), b + md)

        return start, middle, finish

    def sum_mp(quarter, rc, st, rx, group, pack=None):
        b = take(3)
        first, second = 1 - high, high
        s1 = send(quarter(2 * first + 1 - core), rc.at[first], b + first, sib, group)
        s2 = send(quarter(2 * second + 1 - core), rc.at[second], b + second, sib, group)
        cross = send(st, rx, b + 2, opp, group)

        def run():
            s1.start()
            s2.start()
            arrive(rc.at[first], b + first)
            part = quarter(2 * first + core)[...] + rc[first]
            st[...] = part.astype(bf16) if pack is None else pack(part)
            cross.start()
            arrive(rc.at[second], b + second)
            mine = quarter(2 * second + core)[...] + rc[second]
            arrive(rx, b + 2)
            return mine

        return run

    def exchange_x(src_img, dst_img, src_txt, dst_txt):
        b = take(NT)
        ci = [send(src_img(dev[0]), dst_img(ti), b + ti, dev, img_sends) for dev in others_t]
        ct = [send(src_txt(dev[0]), dst_txt, b + 3, dev, txt_sends) for dev in others_t] if src_txt else []

        def start_img():
            for c in ci:
                c.start()

        def start_txt():
            for c in ct:
                c.start()

        def finish():
            for s in range(3):
                @pl.when(t != s)
                def _(s=s):
                    arrive(dst_img(s), b + s)
            if src_txt:
                @pl.when(image)
                def _():
                    arrive(dst_txt, b + 3)

        return start_img, start_txt, finish

    def scatter_dp(sb, rb):
        b = take(ND)
        cs = [send(sb(dd), rb.at[d], b + d, (t, dd, m), all_sends) for dd in others_d]

        def start():
            for c in cs:
                c.start()

        def finish(rows):
            total = sb(d)[...].astype(f32)
            for dd in others_d:
                arrive(rb.at[dd], b + dd)
                total = total + rb[dd].astype(f32)
            return total[:rows]

        return start, finish

    lb = take(5)
    load_xi = pltpu.make_async_copy(img_in.at[0], r["xs"].at[m], sem.at[lb])
    load_xt = pltpu.make_async_copy(txt_in.at[0], r["xt"].at[m], sem.at[lb + 1])
    load_w1 = pltpu.make_async_copy(w1_in, r["w1"], sem.at[lb + 2])
    load_w2 = pltpu.make_async_copy(w2_in, r["w2"], sem.at[lb + 3])
    load_pj = pltpu.make_async_copy(pj_in, r["pj"].at[m], sem.at[lb + 4])
    tw1 = r["w1"].at[pl.ds(0, WT), pl.ds(0, FT)]
    tw2 = r["w2"].at[pl.ds(0, FT), pl.ds(0, WT)]
    load_t1 = pltpu.make_async_copy(tw1_in, tw1, sem.at[lb + 2])
    load_t2 = pltpu.make_async_copy(tw2_in, tw2, sem.at[lb + 3])

    xi_start, xi_mid, xi_fin = gather_mp(lambda i: r["xs"].at[i], img_sends)
    xt_start, xt_mid, xt_fin = gather_mp(lambda i: r["xt"].at[i], txt_sends)
    pj_start, pj_mid, pj_fin = gather_mp(lambda i: r["pj"].at[i], img_sends)

    lab_b = take(3)
    lab_up = send(r["labo"], r["lab"].at[d, ti], lab_b + ti, (NT - 1, d, m), img_sends)
    lab_d = take(ND)
    lab_out = [send(r["lab"].at[d], r["lab"].at[d], lab_d + d, (t, dd, m), txt_sends) for dd in others_d]

    sum2i = sum_mp(lambda q: r["p2i"].at[pl.ds(q * IQ, IQ)], r["rc2i"], r["st2i"], r["rx2i"], img_sends)
    sum2t = sum_mp(lambda q: r["p2t"].at[pl.ds(q * TQ, TQ)], r["rc2t"], r["st2t"], r["rx2t"], txt_sends)

    cols = r["cols"]
    star = take(3)
    star_img = send(r["ei"].at[m], cols.at[d, pl.ds(IQ * ti, IQ)], star + ti, (NT - 1, d, m), img_sends)
    star_txt = [
        send(r["et"].at[m, pl.ds(IQ * c, IQ)], cols.at[d, pl.ds(IQ * c, IQ)], star + c, dev, txt_sends)
        for c in range(3) for dev in others_t
    ]
    ring = take(3 * ND)
    ring_out = [
        [send(cols.at[d, pl.ds(IQ * c, IQ)], cols.at[d, pl.ds(IQ * c, IQ)], ring + ND * c + d, (t, dd, m), all_sends)
         for dd in others_d]
        for c in range(3)
    ]
    ei_start, ei_mid, ei_fin = gather_mp(lambda i: r["ei"].at[i], img_sends)
    et_start, et_mid, et_fin = gather_mp(lambda i: r["et"].at[i], txt_sends)
    bl_start, bl_mid, bl_fin = gather_mp(lambda i: r["bl"].at[i], img_sends)
    hid_si, hid_st, hid_fin = exchange_x(
        lambda s: r["hi"].at[ti], lambda s: r["hi"].at[s], lambda s: r["ht"], r["ht"])
    nor_si, nor_st, nor_fin = exchange_x(
        lambda s: r["ns"].at[s], lambda s: r["an"].at[s], lambda s: r["nt"].at[s], r["ant"])
    blx_si, _, blx_fin = exchange_x(
        lambda s: r["bl"].at[:, s], lambda s: r["al"].at[s], None, None)
    sum4i = sum_mp(lambda q: r["q4t"].at[pl.ds(q * IQ, IQ)], r["rc4t"].at[:, 0:IQ], r["st4t"].at[0:IQ], r["rx4t"].at[0:IQ], img_sends)
    sum4t = sum_mp(lambda q: r["q4t"].at[pl.ds(q * TQ, TQ)], r["rc4t"], r["st4t"], r["rx4t"], txt_sends)
    bi_start, bi_mid, bi_fin = gather_mp(lambda i: r["bfi"].at[i], img_sends)
    bt_start, bt_mid, bt_fin = gather_mp(lambda i: r["bft"].at[i], txt_sends)
    pgb = take(NM)
    pg_out = [
        send(r["pgs"].at[dev[2]], r["pgr"].at[m], pgb + m, dev, img_sends) for dev in (opp, diag, sib)
    ]
    pgx_si, _, pgx_fin = exchange_x(lambda s: r["pgr"], lambda s: r["bj"].at[s], None, None)
    bg_si, bg_st, bg_fin = exchange_x(
        lambda s: r["bsi"].at[s], lambda s: r["ab"].at[s], lambda s: r["bst"].at[s], r["abt"])
    pre_si, pre_st, pre_fin = exchange_x(
        lambda s: r["ki"].at[ti], lambda s: r["ki"].at[s], lambda s: r["kt"], r["kt"])

    def packer(width, full):
        def pack(part):
            rows = part.shape[0]
            tail = part[:, width:]
            lane = lax.broadcasted_iota(jnp.int32, (rows, full - width), 1)
            sums = jnp.sum(jnp.where(lane == 0, tail, 0.0), axis=1, keepdims=True)
            top = sums.astype(bf16).astype(f32)
            low = sums - top
            tail = jnp.where(lane == 0, top, jnp.where(lane == 1, low, 0.0))
            return jnp.concatenate([part[:, :width], tail], axis=1).astype(bf16)
        return pack

    sum6i = sum_mp(lambda q: r["g6i"].at[q], r["rc6i"], r["st6i"], r["rx6i"], img_sends, packer(IS, 512))
    sum6t = sum_mp(lambda q: r["g6t"].at[q], r["rc6t"], r["st6t"], r["rx6t"], txt_sends, packer(TS, 384))
    w2_start, w2_fin = scatter_dp(lambda i: r["sb2"].at[i], r["rb2"])
    t2_start, t2_fin = scatter_dp(lambda i: r["sbt2"].at[i], r["rbt2"])
    j_start, j_fin = scatter_dp(lambda i: r["sbj"].at[i], r["rbj"])
    w1_start, w1_fin = scatter_dp(lambda i: r["w1"].at[pl.ds(i * IP, IP)], r["rb1"])
    t1_start, t1_fin = scatter_dp(lambda i: r["sbt1"].at[i], r["rbt1"])

    @pl.when(image)
    def _():
        load_xi.start()
        load_w1.start()
        load_w2.start()
        load_pj.start()

    @pl.when(text)
    def _():
        load_xt.start()
        load_t1.start()
        load_t2.start()

    barrier = pltpu.get_barrier_semaphore()
    partners = [sib, opp, diag] + others_t + [(t, dd, m) for dd in others_d]
    for dev in partners:
        pl.semaphore_signal(barrier, inc=1, device_id=dev, device_id_type=MESH)
    pl.semaphore_wait(barrier, len(partners))

    @pl.when(image)
    def _():
        load_xi.wait()
        xi_start()
        r["labo"][...] = jnp.full((8, 128), label[0, 0].astype(f32))
        lab_up.start()
        load_pj.wait()
        pj_start()
        xi_mid()
        xi_fin()
        total = jnp.zeros((IR, 1), f32)
        for k in range(NM):
            x = r["xs"][k].astype(f32)
            total = total + jnp.sum(x * x, axis=1, keepdims=True)
        inv = lax.rsqrt(total / WI + epsilon)
        r["ivi"][...] = inv
        for k in range(NM):
            r["ns"][k] = (r["xs"][k].astype(f32) * inv).astype(bf16)
        load_w1.wait()

        def front(j, carry):
            at = pl.ds(pl.multiple_of(j * 384, 384), 384)
            u = dot(r["ns"][0], r["w1"][0:IS, at])
            for k in range(1, NM):
                u = u + dot(r["ns"][k], r["w1"][k * IS:(k + 1) * IS, at])
            val, slope = gelu_both(u)
            r["hi"][ti, :, at] = val.astype(bf16)
            r["gi"][:, at] = slope
            return carry

        lax.fori_loop(0, FI // 384, front, 0)
        load_w2.wait()

        def back(j, carry):
            at = pl.ds(pl.multiple_of(j * 256, 256), 256)
            r["p2i"][:, at] = dot(r["hi"][ti], r["w2"][:, at])
            return carry

        lax.fori_loop(0, WI // 256, back, 0)

    @pl.when(text)
    def _():
        load_xt.wait()
        xt_start()
        xt_mid()
        xt_fin()
        total = jnp.zeros((TR, 1), f32)
        for k in range(NM):
            x = r["xt"][k].astype(f32)
            total = total + jnp.sum(x * x, axis=1, keepdims=True)
        inv = lax.rsqrt(total / WT + epsilon)
        r["ivt"][...] = inv
        for k in range(NM):
            r["nt"][k] = (r["xt"][k].astype(f32) * inv).astype(bf16)
        load_t1.wait()

        def front(j, carry):
            at = pl.ds(pl.multiple_of(j * 128, 128), 128)
            u = dot(r["nt"][0], r["w1"][0:TS, at])
            for k in range(1, NM):
                u = u + dot(r["nt"][k], r["w1"][k * TS:(k + 1) * TS, at])
            val, slope = gelu_both(u)
            r["ht"][:, at] = val.astype(bf16)
            r["gt"][:, at] = slope
            return carry

        lax.fori_loop(0, FT // 128, front, 0)
        load_t2.wait()

        def back(j, carry):
            at = pl.ds(pl.multiple_of(j * 384, 384), 384)
            r["p2t"][:, at] = dot(r["ht"][...], r["w2"][0:FT, at])
            return carry

        lax.fori_loop(0, WT // 384, back, 0)
        for s in range(3):
            arrive(r["lab"].at[d, s], lab_b + s)
        for c in lab_out:
            c.start()

    @pl.when(image)
    def _():
        pj_mid()
        part = sum2i()
        rows = pl.ds(pl.multiple_of(m * IQ, IQ), IQ)
        x = jnp.concatenate([r["xs"][k, rows, :].astype(f32) for k in range(NM)], axis=1)
        blended = (x + (part + r["rx2i"][...].astype(f32))).astype(bf16)
        for k in range(NM):
            r["bl"][m, k] = blended[:, k * IS:(k + 1) * IS]
        pj_fin()
        projected = jnp.concatenate([dot(blended, r["pj"][k]) for k in range(NM)], axis=1)
        length = jnp.sqrt(jnp.sum(projected * projected, axis=1, keepdims=True))
        r["pr"][...] = projected
        r["ln"][...] = length
        r["ei"][m] = (projected / length).astype(bf16)
        star_img.start()
        ei_start()
        bl_start()

    @pl.when(text)
    def _():
        part = sum2t()
        rows = pl.ds(pl.multiple_of(m * TQ, TQ), TQ)
        x = jnp.concatenate([r["xt"][k, rows, :].astype(f32) for k in range(NM)], axis=1)
        blended = x + (part + r["rx2t"][...].astype(f32))
        length = jnp.sqrt(jnp.sum(blended * blended, axis=1, keepdims=True))
        r["tb"][...] = blended
        r["tl"][...] = length
        r["et"][m] = (blended / length).astype(bf16)
        for c in star_txt:
            c.start()
        et_start()

    for c in range(3):
        arrive(cols.at[d, pl.ds(IQ * c, IQ)], star + c)
        for copy in ring_out[c]:
            copy.start()

    @pl.when(image)
    def _():
        ei_mid()
        hid_si()
        nor_si()
        bl_mid()
        ei_fin()

    @pl.when(text)
    def _():
        et_mid()
        hid_st()
        nor_st()
        et_fin()
        for dd in others_d:
            arrive(r["lab"].at[dd], lab_d + dd)

    scale_v, bias_v, loss_v = scale[0, 0], bias[0, 0], loss[0, 0]

    def weight(scores, positive):
        logits = scale_v * scores + bias_v
        signed = jnp.where(positive, 1.0, -1.0).astype(f32)
        grad = -loss_v * signed * jax.nn.sigmoid(-signed * logits)
        return (scale_v * grad).astype(bf16)

    def block_ready(dd):
        for c in range(3):
            arrive(cols.at[dd, pl.ds(IQ * c, IQ)], ring + ND * c + dd)

    @pl.when(image)
    def _():
        emb = r["ei"][...].reshape(IR, WT)
        row = (t * ND + d) * IR + lax.broadcasted_iota(jnp.int32, (IR, TQ), 0) + label[0, 0]
        target = jnp.where(row >= BATCH, row - BATCH, row)
        lane = lax.broadcasted_iota(jnp.int32, (IR, TQ), 1)

        def block(dd):
            pw = weight(dot_t(emb, cols[dd]), target == lane + (dd * TR + m * TQ))
            return dot(pw, cols[dd])

        r["q4t"][0:IR] = block(d)

        def step(k, carry):
            dd = (d + k) % ND
            block_ready(dd)
            r["q4t"][0:IR] += block(dd)
            return carry

        lax.fori_loop(1, ND, step, 0)

    @pl.when(text)
    def _():
        emb = r["et"][...].reshape(TR, WT)
        row = d * TR + lax.broadcasted_iota(jnp.int32, (TR, TQ), 0)
        lane = lax.broadcasted_iota(jnp.int32, (1, TQ), 1)
        part = lane // IQ

        def block(dd):
            off = r["lab"][dd]
            off = jnp.where(part == 0, off[0, :1, :TQ], jnp.where(part == 1, off[1, :1, :TQ], off[2, :1, :TQ]))
            own = (part * ND + dd) * IR + m * IQ + lane % IQ
            target = own + off.astype(jnp.int32)
            target = jnp.where(target >= BATCH, target - BATCH, target)
            pw = weight(dot_t(emb, cols[dd]), row == target)
            return dot(pw, cols[dd])

        r["q4t"][...] = block(d)

        def step(k, carry):
            dd = (d + k) % ND
            block_ready(dd)
            r["q4t"][...] += block(dd)
            return carry

        lax.fori_loop(1, ND, step, 0)

    @pl.when(image)
    def _():
        part = sum4i()
        grad = part + r["rx4t"][0:IQ].astype(f32)
        length = r["ln"][...]
        direction = r["pr"][...] / length
        pg = ((grad - direction * jnp.sum(direction * grad, axis=1, keepdims=True)) / length).astype(bf16)
        blended_grad = jnp.zeros((IQ, WI), f32)
        for k in range(NM):
            piece = pg[:, k * TS:(k + 1) * TS]
            r["pgs"][k] = piece
            blended_grad = blended_grad + dot_t(piece, r["pj"][k])
        r["bfi"][m] = blended_grad.astype(bf16)
        bi_start()
        r["pgr"][m] = r["pgs"][m]
        for c in pg_out:
            c.start()
        bl_fin()
        blx_si()
        r["al"][ti] = r["bl"][:, ti]
        r["an"][ti] = r["ns"][ti]
        bi_mid()
        bi_fin()
        grads = r["bfi"][...].reshape(IR, WI)
        for k in range(NM):
            r["bsi"][k] = grads[:, k * IS:(k + 1) * IS]
        bg_si()
        r["ab"][ti] = r["bsi"][ti]

        def front(j, carry):
            at = pl.ds(pl.multiple_of(j * 384, 384), 384)
            hg = dot_t(r["bfi"][...].reshape(IR, WI), r["w2"][at, :])
            r["ki"][ti, :, at] = (hg * r["gi"][:, at]).astype(bf16)
            return carry

        lax.fori_loop(0, FI // 384, front, 0)
        pre_si()
        for dev in (opp, diag, sib):
            arrive(r["pgr"].at[dev[2]], pgb + dev[2])
        pgx_si()
        r["bj"][ti] = r["pgr"][...]

    @pl.when(text)
    def _():
        part = sum4t()
        grad = part + r["rx4t"][...].astype(f32)
        length = r["tl"][...]
        direction = r["tb"][...] / length
        blended_grad = (grad - direction * jnp.sum(direction * grad, axis=1, keepdims=True)) / length
        r["bft"][m] = blended_grad.astype(bf16)
        bt_start()
        r["ant"][...] = r["nt"][NT - 1]
        bt_mid()
        bt_fin()
        grads = r["bft"][...].reshape(TR, WT)
        for k in range(NM):
            r["bst"][k] = grads[:, k * TS:(k + 1) * TS]
        bg_st()
        r["abt"][...] = r["bst"][NT - 1]

        def front(j, carry):
            at = pl.ds(pl.multiple_of(j * 128, 128), 128)
            hg = dot_t(r["bft"][...].reshape(TR, WT), r["w2"][at, 0:WT])
            r["kt"][:, at] = (hg * r["gt"][:, at]).astype(bf16)
            return carry

        lax.fori_loop(0, FT // 128, front, 0)
        pre_st()

    def product(a, b_ref, sb, rows, padded, width, lead):
        def tile(j, carry):
            at = pl.ds(pl.multiple_of(j * width, width), width)
            b = b_ref[:, :, at].reshape(lead, width) if len(b_ref.shape) == 3 else b_ref[:, at]
            g = dot_rows(a, b)
            pad = jnp.zeros((padded - rows, width), f32)
            for dd in range(ND):
                piece = jnp.concatenate([g[dd * rows:(dd + 1) * rows], pad], axis=0)
                sb(dd)[:, at] = piece.astype(bf16)
            return carry

        lax.fori_loop(0, b_ref.shape[-1] // width, tile, 0)

    hid_fin()
    bg_fin()
    product(r["ab"][...].reshape(3 * IR, IS), r["hi"], lambda i: r["sb2"].at[i], IO, IP, 384, 3 * IR)
    w2_start()
    product(r["abt"][...], r["ht"], lambda i: r["sbt2"].at[i], TO, TP, 128, TR)
    t2_start()

    @pl.when(image)
    def _():
        total = jnp.zeros((IR, 1), f32)
        inv = r["ivi"][...]
        lane = lax.broadcasted_iota(jnp.int32, (IR, 512 - IS), 1)
        for k in range(NM):
            g = dot_t(r["ki"][ti], r["w1"][k * IS:(k + 1) * IS, :])
            total = total + jnp.sum(r["xs"][k].astype(f32) * inv * g, axis=1, keepdims=True)
            r["g6i"][k, :, 0:IS] = g
        tail = jnp.where(lane == 0, total, 0.0)
        for k in range(NM):
            r["g6i"][k, :, IS:512] = tail
        part = sum6i()
        other = r["rx6i"][...].astype(f32)
        sums = part[:, IS:] + other[:, IS:]
        sums = jnp.where(lane == 0, sums, jnp.where(lane == 1, other[:, IS:], 0.0))
        average = jnp.sum(sums, axis=1, keepdims=True) / WI
        grad = part[:, :IS] + other[:, :IS]
        normed = r["xs"][m].astype(f32) * inv
        o_img[0] = r["bsi"][m].astype(f32) + (grad - normed * average) * inv
        o_txt[0] = jnp.zeros((TR, TS), f32)

    @pl.when(text)
    def _():
        total = jnp.zeros((TR, 1), f32)
        inv = r["ivt"][...]
        lane = lax.broadcasted_iota(jnp.int32, (TR, 384 - TS), 1)
        for k in range(NM):
            g = dot_t(r["kt"][...], r["w1"][k * TS:(k + 1) * TS, 0:FT])
            total = total + jnp.sum(r["xt"][k].astype(f32) * inv * g, axis=1, keepdims=True)
            r["g6t"][k, :, 0:TS] = g
        tail = jnp.where(lane == 0, total, 0.0)
        for k in range(NM):
            r["g6t"][k, :, TS:384] = tail
        part = sum6t()
        other = r["rx6t"][...].astype(f32)
        sums = part[:, TS:] + other[:, TS:]
        sums = jnp.where(lane == 0, sums, jnp.where(lane == 1, other[:, TS:], 0.0))
        average = jnp.sum(sums, axis=1, keepdims=True) / WT
        grad = part[:, :TS] + other[:, :TS]
        normed = r["xt"][m].astype(f32) * inv
        o_txt[0] = r["bst"][m].astype(f32) + (grad - normed * average) * inv
        o_img[0] = jnp.zeros((IR, IS), f32)

    blx_fin()
    pgx_fin()
    b = r["bj"][...].reshape(3 * IR, TS)
    g = dot_rows(r["al"][...].reshape(3 * IR, IS), b)
    pad = jnp.zeros((IP - IO, TS), f32)
    for dd in range(ND):
        r["sbj"][dd] = jnp.concatenate([g[dd * IO:(dd + 1) * IO], pad], axis=0).astype(bf16)
    j_start()
    nor_fin()
    pre_fin()
    product(r["an"][...].reshape(3 * IR, IS), r["ki"], lambda i: r["w1"].at[pl.ds(i * IP, IP)], IO, IP, 384, 3 * IR)
    w1_start()
    product(r["ant"][...], r["kt"], lambda i: r["sbt1"].at[i], TO, TP, 128, TR)
    t1_start()

    o_w2[...] = w2_fin(IO)
    o_t2[...] = t2_fin(TO)
    o_pj[...] = j_fin(IO)
    o_w1[...] = w1_fin(IO)
    o_t1[...] = t1_fin(TO)

    for c in all_sends:
        c.wait_send()

    @pl.when(image)
    def _():
        for c in img_sends:
            c.wait_send()

    @pl.when(text)
    def _():
        for c in txt_sends:
            c.wait_send()


def per_device(
    image_in, text_in, img_w1, img_w2, img_proj, txt_w1, txt_w2, label_offset,
    logit_scale, logit_bias, loss_scale,
):
    anywhere = pl.BlockSpec(memory_space=pl.ANY)
    scalar = pl.BlockSpec(memory_space=pltpu.SMEM)
    vmem = pl.BlockSpec(memory_space=pltpu.VMEM)
    one = lambda v: v.reshape(1, 1)
    outs = pl.pallas_call(
        step_kernel,
        out_shape=[
            jax.ShapeDtypeStruct((1, IR, IS), f32),
            jax.ShapeDtypeStruct((1, TR, TS), f32),
            jax.ShapeDtypeStruct((IO, FI), f32),
            jax.ShapeDtypeStruct((IO, FI), f32),
            jax.ShapeDtypeStruct((IO, TS), f32),
            jax.ShapeDtypeStruct((TO, FT), f32),
            jax.ShapeDtypeStruct((TO, FT), f32),
        ],
        in_specs=[anywhere] * 7 + [scalar] * 4,
        out_specs=[vmem] * 7,
        scratch_shapes=list(scratch_list().values()),
        compiler_params=pltpu.CompilerParams(
            collective_id=0, has_side_effects=True, vmem_limit_bytes=63 << 20
        ),
        name="step",
    )(
        image_in, text_in, img_w1, img_w2, img_proj, txt_w1, txt_w2, label_offset,
        one(logit_scale), one(logit_bias), one(loss_scale),
    )
    g_img, g_txt, g_w1, g_w2, g_pj, g_t1, g_t2 = outs
    return (g_img, g_txt, g_w1, g_w2.T, g_pj, g_t1, g_t2.T)


def solution(mesh):
    return jax.shard_map(
        per_device,
        mesh=mesh,
        in_specs=(
            P("tower", "dp", "mp"),
            P("tower", "dp", "mp"),
            P(None, "mp"),
            P("mp", None),
            P(None, "mp"),
            P(None, "mp"),
            P("mp", None),
            P("tower", "dp"),
            P(),
            P(),
            P(),
        ),
        out_specs=(
            P("tower", "dp", "mp"),
            P("tower", "dp", "mp"),
            P(("tower", "dp"), "mp"),
            P("mp", ("tower", "dp")),
            P(("tower", "dp"), "mp"),
            P(("tower", "dp"), "mp"),
            P("mp", ("tower", "dp")),
        ),
        check_vma=False,
    )
```

time: 1030 us -> 210 us (0.20)
  the two profiles are of different devices: /device:TPU:0 before, /device:TPU:12 now
where the time goes in v1:
time: 210 us; the launch traced here: 207 us
  Pallas kernels  191 us (91%)
  local copies, waits for them, and re-layouts  13.3 us (6%)
  between operations  3.25 us (2%)
    pallas_call x1, Pallas kernels, per_device(): pl.pallas_call(step_kernel, out_shape=[jax.ShapeDtypeStruct((1, IR, IS),...  191 us
    unnamed x20, local copies, waits for them, and re-layouts  13.3 us

profile of v1, /device:TPU:12, one launch (start us, length us, event | category | flops | bytes accessed | tf_op | source)
XLA Modules:
  0.0 207.4 jit_solution(1372202716395561477)
XLA Ops:
  3.2 1.7 copy.18.img_in
  4.9 1.8 copy.19.txt_in
  6.7 2.5 %copy.20.pj_in = bf16[1792,288]{1,0:T(8,128)(2,1)} copy(bf16[1792,288]{0,1:T(8,128)(2,1)} %param.15) | data formatting | bytes 2064384 | tf_op args[4]
  9.2 190.8 %step.1 = (f32[1,128,448]{2,1,0:T(8,128)}, f32[1,384,288]{2,1,0:T(8,128)}, f32[56,1920]{1,0:T(8,128)}, f32[56,1920]{1,0:T(8,128)}, f32[56,288]{1,0:T(8,128)}, /*index=5*/f32[36,640]{1,0:T(8,128)}, f32[36,640]{1,0:T(8,128)}) custom-call(bf16[1,128,448]{2,1,0:T(8,128)(2,1)} %copy.18.img_in, bf16[1,384,288]{2,1,0:T(8,128)(2,1)} %copy.19.txt_in, ...), custom_call_target="tpu_custom_call" | custom-call | tf_op jit(solution)/shard_map/step/pallas_call | solution.py:731
  200.0 0.0 copy-start.1
  200.0 0.0 copy-start
  200.0 1.8 copy.21
  201.8 0.0 copy-start.4
  201.8 0.0 copy-start.3
  201.8 0.0 copy-start.2
  201.8 2.1 %copy.22 = f32[1,384,288]{1,2,0:T(8,128)} copy(f32[1,384,288]{2,1,0:T(8,128)} %get-tuple-element.22) | data formatting | bytes 884736
  203.9 0.0 copy-done.1
  203.9 0.8 copy.32
  204.7 0.0 copy-done
  204.7 0.8 copy.33
  205.4 0.0 copy-done.4
  205.4 0.6 copy.34
  206.1 0.0 copy-done.3
  206.1 0.6 copy.35
  206.7 0.0 copy-done.2
  206.7 0.6 copy.36
Async XLA Ops:
  200.0 4.0 %copy-start.1 = (f32[56,1920]{1,0:T(8,128)S(1)}, f32[56,1920]{1,0:T(8,128)}, u32[]{:S(2)}) copy-start(f32[56,1920]{1,0:T(8,128)} %get-tuple-element.37) | copy-start | bytes 1290244
  200.0 4.7 %copy-start = (f32[56,1920]{1,0:T(8,128)S(1)}, f32[56,1920]{1,0:T(8,128)}, u32[]{:S(2)}) copy-start(f32[56,1920]{1,0:T(8,128)} %get-tuple-element.17) | copy-start | bytes 1290244
  201.8 3.6 %copy-start.4 = (f32[56,288]{1,0:T(8,128)S(1)}, f32[56,288]{1,0:T(8,128)}, u32[]{:S(2)}) copy-start(f32[56,288]{1,0:T(8,128)} %get-tuple-element.39) | copy-start | bytes 193540
  201.8 4.2 %copy-start.3 = (f32[36,640]{1,0:T(8,128)S(1)}, f32[36,640]{1,0:T(8,128)}, u32[]{:S(2)}) copy-start(f32[36,640]{1,0:T(8,128)} %get-tuple-element.40) | copy-start | bytes 276484
  201.8 4.9 %copy-start.2 = (f32[36,640]{1,0:T(8,128)S(1)}, f32[36,640]{1,0:T(8,128)}, u32[]{:S(2)}) copy-start(f32[36,640]{1,0:T(8,128)} %get-tuple-element.20) | copy-start | bytes 276484

commit v2 on v1

v2 whole, which is shorter than its diff:
```python
import functools
import math

import jax
import jax.numpy as jnp
from jax import lax
from jax.experimental import pallas as pl
from jax.experimental.pallas import tpu as pltpu
from jax.sharding import PartitionSpec as P

epsilon = 1e-06
bf16 = jnp.bfloat16
f32 = jnp.float32
MESH = pl.DeviceIdType.MESH
GELU_A = math.sqrt(2.0 / math.pi)
GELU_B = 0.044715

NT = 4
ND = 8
NM = 4
IR = 128
TR = 384
IQ = IR // NM
TQ = TR // NM
WI = 1792
WT = 1152
IS = WI // NM
TS = WT // NM
FI = 1920
FT = 640
BATCH = 3072
IO = WI // 32
TO = WT // 32
IP = 64
TP = 48
IG = IS + 16
TG = TS + 16
FC = 640
N_SEM = 420
LIMIT = None


def dot(a, b):
    return jnp.dot(a, b, preferred_element_type=f32)


def dot_t(a, b):
    return lax.dot_general(a, b, (((1,), (1,)), ((), ())), preferred_element_type=f32)


def dot_rows(a, b):
    return lax.dot_general(a, b, (((0,), (0,)), ((), ())), preferred_element_type=f32)


def gelu_both(u):
    sq = u * u
    th = jnp.tanh(GELU_A * u * (1.0 + GELU_B * sq))
    half = 0.5 * (1.0 + th)
    slope = half + 0.5 * u * (1.0 - th * th) * (GELU_A * (1.0 + 3.0 * GELU_B * sq))
    return u * half, slope


def scratch_list():
    v = pltpu.VMEM
    return dict(
        w1=v((WI, FI), bf16),
        w2=v((FI, WI), bf16),
        pj=v((WT, WI), bf16),
        xs=v((WI, IR), bf16),
        xt=v((WT, TR), bf16),
        xf=v((IR, WI), bf16),
        xtf=v((TR, WT), bf16),
        ns=v((WI, IR), bf16),
        nt=v((WT, TR), bf16),
        nf=v((IR, WI), bf16),
        ntf=v((TR, WT), bf16),
        ivi=v((1, IR), f32),
        ivt=v((1, TR), f32),
        hi=v((3, IR, FI), bf16),
        ht=v((TR, FT), bf16),
        gi=v((IR, FI), f32),
        gt=v((TR, FT), f32),
        p2i=v((IR, WI), f32),
        p2t=v((TR, WT), f32),
        rc2i=v((2, IQ, WI), f32),
        rc2t=v((2, TQ, WT), f32),
        st2i=v((IQ, WI), bf16),
        st2t=v((TQ, WT), bf16),
        rx2i=v((IQ, WI), bf16),
        rx2t=v((TQ, WT), bf16),
        tb=v((TQ, WT), f32),
        tl=v((TQ, 1), f32),
        bl=v((NM, NM, IQ, IS), bf16),
        pr=v((IQ, WT), f32),
        ln=v((IQ, 1), f32),
        ei=v((NM, IQ, WT), bf16),
        et=v((NM, TQ, WT), bf16),
        cols=v((ND, TQ, WT), bf16),
        lab=v((ND, 3, 8, 128), f32),
        labo=v((8, 128), f32),
        q4t=v((TR, WT), f32),
        rc4t=v((2, TQ, WT), f32),
        st4t=v((TQ, WT), bf16),
        rx4t=v((TQ, WT), bf16),
        bfi=v((NM, IQ, WI), bf16),
        bft=v((NM, TQ, WT), bf16),
        pgf=v((IQ, WT), bf16),
        pgs=v((NM, IQ, TS), bf16),
        pgr=v((NM, IQ, TS), bf16),
        bsi=v((WI, IR), bf16),
        bst=v((WT, TR), bf16),
        an=v((3, IS, IR), bf16),
        ant=v((TS, TR), bf16),
        ab=v((3, IS, IR), bf16),
        abt=v((TS, TR), bf16),
        al=v((3, NM, IQ, IS), bf16),
        bj=v((3, NM, IQ, TS), bf16),
        ki=v((3, IR, FI), bf16),
        kt=v((TR, FT), bf16),
        g6i=v((NM, IG, IR), f32),
        g6t=v((NM, TG, TR), f32),
        rc6i=v((2, IG, IR), f32),
        rc6t=v((2, TG, TR), f32),
        st6i=v((IG, IR), bf16),
        st6t=v((TG, TR), bf16),
        rx6i=v((IG, IR), bf16),
        rx6t=v((TG, TR), bf16),
        ra1=v((2, 4 * IO, FI), bf16),
        sc1=v((4, IP, FI), bf16),
        rc1=v((4, IP, FI), bf16),
        ra2=v((4, 2 * IO, FI), bf16),
        sc2=v((2, IP, FI), bf16),
        rc2=v((2, IP, FI), bf16),
        sbj=v((2, 4 * IO, TS), bf16),
        raj=v((2, 4 * IO, TS), bf16),
        scj=v((4, IP, TS), bf16),
        rcj=v((4, IP, TS), bf16),
        sbt1=v((4, 2 * TO, FT), bf16),
        rat1=v((4, 2 * TO, FT), bf16),
        sct1=v((2, TP, FT), bf16),
        rct1=v((2, TP, FT), bf16),
        sbt2=v((2, 4 * TO, FT), bf16),
        rat2=v((2, 4 * TO, FT), bf16),
        sct2=v((4, TP, FT), bf16),
        rct2=v((4, TP, FT), bf16),
        sem=pltpu.SemaphoreType.DMA((N_SEM,)),
    )


NAMES = list(scratch_list())


def step_kernel(
    img_in, txt_in, w1_in, w2_in, pj_in, tw1_in, tw2_in, label, scale, bias, loss,
    o_img, o_txt, o_w1, o_w2, o_pj, o_t1, o_t2, *scratch
):
    r = dict(zip(NAMES, scratch))
    sem = r["sem"]
    used = [0]
    t = lax.axis_index("tower")
    d = lax.axis_index("dp")
    m = lax.axis_index("mp")
    core = m % 2
    high = m // 2
    ms = m + 1 - 2 * core
    mo = (m + 2) % NM
    md = (ms + 2) % NM
    text = t == NT - 1
    image = t != NT - 1
    ti = jnp.minimum(t, 2)
    sib, opp, diag = (t, d, ms), (t, d, mo), (t, d, md)
    dy = d // 4
    dz = d % 4
    others_t = [((t + k) % NT, d, m) for k in (1, 2, 3)]
    order_d = (4, 1, 3, 5, 7, 2, 6)
    others_d = [(d + k) % ND for k in order_d]

    def take(n):
        first = used[0]
        used[0] += n
        assert used[0] <= N_SEM
        return first

    img_sends, txt_sends, all_sends = [], [], []
    plans = []

    class Tracked:
        def __init__(self, copy, group):
            self.copy, self.group = copy, group

        def start(self):
            self.copy.start()
            self.group.append(self.copy)

    def plan(group, *steps):
        entry = {"group": group, "left": list(steps), "begun": False}
        plans.append(entry)

        def runner(step):
            def run(*args):
                entry["begun"] = True
                entry["left"].remove(step)
                return step(*args)
            return run

        return [runner(s) for s in steps]

    def send(src, dst, arrived, dev, group):
        copy = pltpu.make_async_remote_copy(
            src_ref=src, dst_ref=dst, send_sem=sem.at[take(1)], recv_sem=sem.at[arrived],
            device_id=dev, device_id_type=MESH,
        )
        return Tracked(copy, group)

    def arrive(dst, arrived):
        pltpu.make_async_remote_copy(
            src_ref=dst, dst_ref=dst, send_sem=sem.at[0], recv_sem=sem.at[arrived],
            device_id=sib, device_id_type=MESH,
        ).wait_recv()

    def gather_mp(slot, group):
        b = take(NM)
        to_opp = send(slot(m), slot(m), b + m, opp, group)
        to_sib = send(slot(m), slot(m), b + m, sib, group)
        pass_on = send(slot(mo), slot(mo), b + mo, sib, group)

        def start():
            to_opp.start()
            to_sib.start()

        def middle():
            arrive(slot(mo), b + mo)
            pass_on.start()

        def finish():
            arrive(slot(ms), b + ms)
            arrive(slot(md), b + md)

        return plan(group, start, middle, finish)

    def sum_mp(quarter, rc, st, rx, group, pack=None):
        b = take(3)
        first, second = 1 - high, high
        s1 = send(quarter(2 * first + 1 - core), rc.at[first], b + first, sib, group)
        s2 = send(quarter(2 * second + 1 - core), rc.at[second], b + second, sib, group)
        cross = send(st, rx, b + 2, opp, group)

        def start():
            s1.start()
            s2.start()

        def middle():
            arrive(rc.at[first], b + first)
            part = quarter(2 * first + core)[...] + rc[first]
            st[...] = part.astype(bf16) if pack is None else pack(part)
            cross.start()

        def finish():
            arrive(rc.at[second], b + second)
            mine = quarter(2 * second + core)[...] + rc[second]
            arrive(rx, b + 2)
            return mine

        return plan(group, start, middle, finish)

    def exchange_x(src_img, dst_img, src_txt, dst_txt):
        b = take(NT)
        ci = [send(src_img(dev[0]), dst_img(ti), b + ti, dev, img_sends) for dev in others_t]
        ct = [send(src_txt(dev[0]), dst_txt, b + 3, dev, txt_sends) for dev in others_t] if src_txt else []

        def start_img():
            for c in ci:
                c.start()

        def start_txt():
            for c in ct:
                c.start()

        def finish():
            for s in range(3):
                @pl.when(t != s)
                def _(s=s):
                    arrive(dst_img(s), b + s)
            if src_txt:
                @pl.when(image)
                def _():
                    arrive(dst_txt, b + 3)

        return plan(all_sends, start_img, start_txt, finish)

    def scatter_dp(mode, own, padded, spans, first, first_in, second, second_in):
        along_y = mode == "y"
        parts = 2 if along_y else 4
        me, rest = (dy, dz) if along_y else (dz, dy)

        def dev_first(p):
            return (t, p * 4 + dz, m) if along_y else (t, dy * 4 + p, m)

        def dev_second(p):
            return (t, dy * 4 + p, m) if along_y else (t, p * 4 + dz, m)

        steps = []
        for j, span in enumerate(spans):
            b1, b2 = take(4), take(4)
            one = [(me + k) % parts for k in range(1, parts)]
            two = [(rest + k) % (8 // parts) for k in range(1, 8 // parts)]
            c1 = [send(first(j, p), first_in.at[me, :, span], b1 + me, dev_first(p), all_sends) for p in one]
            c2 = [send(second.at[p, :, span], second_in.at[rest, :, span], b2 + rest, dev_second(p), all_sends)
                  for p in two]

            def start(c1=c1):
                for c in c1:
                    c.start()

            def middle(j=j, span=span, one=one, b1=b1, c2=c2):
                total = first(j, me)[...].astype(f32)
                for p in one:
                    arrive(first_in.at[p, :, span], b1 + p)
                    total = total + first_in[p, :, span].astype(f32)
                pad = jnp.zeros((padded - own, total.shape[1]), f32)
                for k in range(8 // parts):
                    piece = jnp.concatenate([total[k * own:(k + 1) * own], pad], axis=0)
                    second[k, :, span] = piece.astype(bf16)
                for c in c2:
                    c.start()

            def finish(out=None, span=span, two=two, b2=b2):
                total = second[rest, :, span].astype(f32)
                for p in two:
                    arrive(second_in.at[p, :, span], b2 + p)
                    total = total + second_in[p, :, span].astype(f32)
                if out is not None:
                    out[:, span] = total[:own]

            steps.append(plan(all_sends, start, middle, finish))
        return steps

    lb = take(5)
    mi = pl.ds(pl.multiple_of(m * IS, IS), IS)
    mt = pl.ds(pl.multiple_of(m * TS, TS), TS)
    load_xi = pltpu.make_async_copy(img_in.at[0], r["xs"].at[mi], sem.at[lb])
    load_xt = pltpu.make_async_copy(txt_in.at[0], r["xt"].at[mt], sem.at[lb + 1])
    load_w1 = pltpu.make_async_copy(w1_in, r["w1"], sem.at[lb + 2])
    load_w2 = pltpu.make_async_copy(w2_in, r["w2"], sem.at[lb + 3])
    load_pj = pltpu.make_async_copy(pj_in, r["pj"].at[mt], sem.at[lb + 4])
    tw1 = r["w1"].at[pl.ds(0, WT), pl.ds(0, FT)]
    tw2 = r["w2"].at[pl.ds(0, FT), pl.ds(0, WT)]
    load_t1 = pltpu.make_async_copy(tw1_in, tw1, sem.at[lb + 2])
    load_t2 = pltpu.make_async_copy(tw2_in, tw2, sem.at[lb + 3])

    xi_start, xi_mid, xi_fin = gather_mp(lambda i: r["xs"].at[pl.ds(pl.multiple_of(i * IS, IS), IS)], img_sends)
    xt_start, xt_mid, xt_fin = gather_mp(lambda i: r["xt"].at[pl.ds(pl.multiple_of(i * TS, TS), TS)], txt_sends)
    pj_start, pj_mid, pj_fin = gather_mp(lambda i: r["pj"].at[pl.ds(pl.multiple_of(i * TS, TS), TS)], img_sends)

    lab_b = take(3)
    lab_up = send(r["labo"], r["lab"].at[d, ti], lab_b + ti, (NT - 1, d, m), img_sends)
    lab_d = take(ND)
    lab_out = [send(r["lab"].at[d], r["lab"].at[d], lab_d + d, (t, dd, m), txt_sends) for dd in others_d]

    s2i_start, s2i_mid, s2i_fin = sum_mp(lambda q: r["p2i"].at[pl.ds(q * IQ, IQ)], r["rc2i"], r["st2i"], r["rx2i"], img_sends)
    s2t_start, s2t_mid, s2t_fin = sum_mp(lambda q: r["p2t"].at[pl.ds(q * TQ, TQ)], r["rc2t"], r["st2t"], r["rx2t"], txt_sends)

    cols = r["cols"]
    star = take(3)
    star_img = send(r["ei"].at[m], cols.at[d, pl.ds(IQ * ti, IQ)], star + ti, (NT - 1, d, m), img_sends)
    star_txt = [
        send(r["et"].at[m, pl.ds(IQ * c, IQ)], cols.at[d, pl.ds(IQ * c, IQ)], star + c, dev, txt_sends)
        for c in range(3) for dev in others_t
    ]
    ring = take(3 * ND)
    ring_out = [
        [send(cols.at[d, pl.ds(IQ * c, IQ)], cols.at[d, pl.ds(IQ * c, IQ)], ring + ND * c + d, (t, dd, m), all_sends)
         for dd in others_d]
        for c in range(3)
    ]
    ei_start, ei_mid, ei_fin = gather_mp(lambda i: r["ei"].at[i], img_sends)
    et_start, et_mid, et_fin = gather_mp(lambda i: r["et"].at[i], txt_sends)
    bl_start, bl_mid, bl_fin = gather_mp(lambda i: r["bl"].at[i], img_sends)
    hid_si, hid_st, hid_fin = exchange_x(
        lambda s: r["hi"].at[ti], lambda s: r["hi"].at[s], lambda s: r["ht"], r["ht"])
    nor_si, nor_st, nor_fin = exchange_x(
        lambda s: r["ns"].at[pl.ds(s * IS, IS)], lambda s: r["an"].at[s], lambda s: r["nt"].at[pl.ds(s * TS, TS)], r["ant"])
    blx_si, _, blx_fin = exchange_x(
        lambda s: r["bl"].at[:, s], lambda s: r["al"].at[s], None, None)
    s4i_start, s4i_mid, s4i_fin = sum_mp(lambda q: r["q4t"].at[pl.ds(q * IQ, IQ)], r["rc4t"].at[:, 0:IQ], r["st4t"].at[0:IQ], r["rx4t"].at[0:IQ], img_sends)
    s4t_start, s4t_mid, s4t_fin = sum_mp(lambda q: r["q4t"].at[pl.ds(q * TQ, TQ)], r["rc4t"], r["st4t"], r["rx4t"], txt_sends)
    bi_start, bi_mid, bi_fin = gather_mp(lambda i: r["bfi"].at[i], img_sends)
    bt_start, bt_mid, bt_fin = gather_mp(lambda i: r["bft"].at[i], txt_sends)
    pgb = take(NM)
    pg_out = [
        send(r["pgs"].at[dev[2]], r["pgr"].at[m], pgb + m, dev, img_sends) for dev in (opp, diag, sib)
    ]
    pgx_si, _, pgx_fin = exchange_x(lambda s: r["pgr"], lambda s: r["bj"].at[s], None, None)
    bg_si, bg_st, bg_fin = exchange_x(
        lambda s: r["bsi"].at[pl.ds(s * IS, IS)], lambda s: r["ab"].at[s], lambda s: r["bst"].at[pl.ds(s * TS, TS)], r["abt"])
    pre = []
    for j in range(FI // FC):
        at = slice(j * FC, (j + 1) * FC)
        pre.append(exchange_x(
            lambda s, at=at: r["ki"].at[ti, :, at], lambda s, at=at: r["ki"].at[s, :, at],
            (lambda s: r["kt"]) if j == 0 else None, r["kt"]))

    def packer(width):
        def pack(part):
            sums = part[width:]
            top = sums.astype(bf16).astype(f32)
            at = lax.broadcasted_iota(jnp.int32, sums.shape, 0)
            tail = jnp.where(at == 1, sums[0:1] - top[0:1], top)
            return jnp.concatenate([part[:width], tail], axis=0).astype(bf16)
        return pack

    s6i_start, s6i_mid, s6i_fin = sum_mp(lambda q: r["g6i"].at[q], r["rc6i"], r["st6i"], r["rx6i"], img_sends, packer(IS))
    s6t_start, s6t_mid, s6t_fin = sum_mp(lambda q: r["g6t"].at[q], r["rc6t"], r["st6t"], r["rx6t"], txt_sends, packer(TS))
    spans = [slice(j * FC, (j + 1) * FC) for j in range(FI // FC)]
    whole_t = [slice(0, FT)]
    whole_j = [slice(0, TS)]
    def sb2(j, p):
        return r["w2"].at[pl.ds(pl.multiple_of(j * 8 * IO + p * 2 * IO, 2 * IO), 2 * IO), 0:FC]

    def sb1(j, p):
        return r["w1"].at[pl.ds(pl.multiple_of(p * 4 * IO, 4 * IO), 4 * IO), spans[j]]

    w2_steps = scatter_dp(
        "z", IO, IP, spans, sb2, r["ra2"], r["sc2"], r["rc2"])
    w1_steps = scatter_dp(
        "y", IO, IP, spans, sb1, r["ra1"], r["sc1"], r["rc1"])
    t2_steps = scatter_dp("y", TO, TP, whole_t, lambda j, p: r["sbt2"].at[p], r["rat2"], r["sct2"], r["rct2"])
    t1_steps = scatter_dp("z", TO, TP, whole_t, lambda j, p: r["sbt1"].at[p], r["rat1"], r["sct1"], r["rct1"])
    pj_steps = scatter_dp("y", IO, IP, whole_j, lambda j, p: r["sbj"].at[p], r["raj"], r["scj"], r["rcj"])

    @pl.when(image)
    def _():
        load_xi.start()
        load_w1.start()
        load_w2.start()
        load_pj.start()

    @pl.when(text)
    def _():
        load_xt.start()
        load_t1.start()
        load_t2.start()

    barrier = pltpu.get_barrier_semaphore()
    partners = [sib, opp, diag] + others_t + [(t, dd, m) for dd in others_d]
    for dev in partners:
        pl.semaphore_signal(barrier, inc=1, device_id=dev, device_id_type=MESH)
    pl.semaphore_wait(barrier, len(partners))

    @pl.when(image)
    def _():
        load_xi.wait()
        xi_start()
        r["labo"][...] = jnp.full((8, 128), label[0, 0].astype(f32))
        lab_up.start()
        load_pj.wait()
        pj_start()
        xi_mid()
        xi_fin()
        xt32 = r["xs"][...].astype(f32)
        inv = lax.rsqrt(jnp.sum(xt32 * xt32, axis=0, keepdims=True) / WI + epsilon)
        r["ivi"][...] = inv
        r["ns"][...] = (xt32 * inv).astype(bf16)
        r["nf"][...] = r["ns"][...].T

    @pl.when(text)
    def _():
        load_xt.wait()
        xt_start()
        xt_mid()
        xt_fin()
        xt32 = r["xt"][...].astype(f32)
        inv = lax.rsqrt(jnp.sum(xt32 * xt32, axis=0, keepdims=True) / WT + epsilon)
        r["ivt"][...] = inv
        r["nt"][...] = (xt32 * inv).astype(bf16)
        r["ntf"][...] = r["nt"][...].T

    @pl.when(image)
    def _():
        load_w1.wait()

        def front(j, carry):
            at = pl.ds(pl.multiple_of(j * 384, 384), 384)
            u = dot(r["nf"][...], r["w1"][:, at])
            val, slope = gelu_both(u)
            r["hi"][ti, :, at] = val.astype(bf16)
            r["gi"][:, at] = slope
            return carry

        lax.fori_loop(0, FI // 384, front, 0)

    @pl.when(text)
    def _():
        load_t1.wait()

        for at in (slice(0, 256), slice(256, 512), slice(512, 640)):
            val, slope = gelu_both(dot(r["ntf"][...], r["w1"][0:WT, at]))
            r["ht"][:, at] = val.astype(bf16)
            r["gt"][:, at] = slope

    @pl.when(image)
    def _():
        load_w2.wait()

        def back(j, carry):
            at = pl.ds(pl.multiple_of(j * 256, 256), 256)
            r["p2i"][:, at] = dot(r["hi"][ti], r["w2"][:, at])
            return carry

        lax.fori_loop(0, WI // 256, back, 0)

    @pl.when(text)
    def _():
        load_t2.wait()

        def back(j, carry):
            at = pl.ds(pl.multiple_of(j * 384, 384), 384)
            r["p2t"][:, at] = dot(r["ht"][...], r["w2"][0:FT, at])
            return carry

        lax.fori_loop(0, WT // 384, back, 0)
        for s in range(3):
            arrive(r["lab"].at[d, s], lab_b + s)
        for c in lab_out:
            c.start()

    @pl.when(image)
    def _():
        r["xf"][...] = r["xs"][...].T
        s2i_start()
        s2i_mid()
        part = s2i_fin()
        rows = pl.ds(pl.multiple_of(m * IQ, IQ), IQ)
        x = r["xf"][rows, :].astype(f32)
        blended = (x + (part + r["rx2i"][...].astype(f32))).astype(bf16)
        for k in range(NM):
            r["bl"][m, k] = blended[:, k * IS:(k + 1) * IS]
        pj_mid()
        pj_fin()
        projected = dot_t(blended, r["pj"][...])
        length = jnp.sqrt(jnp.sum(projected * projected, axis=1, keepdims=True))
        r["pr"][...] = projected
        r["ln"][...] = length
        r["ei"][m] = (projected / length).astype(bf16)
        star_img.start()
        ei_start()
        bl_start()

    @pl.when(text)
    def _():
        r["xtf"][...] = r["xt"][...].T
        s2t_start()
        s2t_mid()
        part = s2t_fin()
        rows = pl.ds(pl.multiple_of(m * TQ, TQ), TQ)
        x = r["xtf"][rows, :].astype(f32)
        blended = x + (part + r["rx2t"][...].astype(f32))
        length = jnp.sqrt(jnp.sum(blended * blended, axis=1, keepdims=True))
        r["tb"][...] = blended
        r["tl"][...] = length
        r["et"][m] = (blended / length).astype(bf16)
        for c in star_txt:
            c.start()
        et_start()

    for c in range(3):
        arrive(cols.at[d, pl.ds(IQ * c, IQ)], star + c)
        for copy in ring_out[c]:
            copy.start()

    @pl.when(image)
    def _():
        ei_mid()
        hid_si()
        nor_si()
        bl_mid()
        ei_fin()

    @pl.when(text)
    def _():
        et_mid()
        hid_st()
        nor_st()
        et_fin()
        for dd in others_d:
            arrive(r["lab"].at[dd], lab_d + dd)

    scale_v, bias_v, loss_v = scale[0, 0], bias[0, 0], loss[0, 0]

    def weight(scores, positive):
        logits = scale_v * scores + bias_v
        signed = jnp.where(positive, 1.0, -1.0).astype(f32)
        grad = -loss_v * signed * jax.nn.sigmoid(-signed * logits)
        return (scale_v * grad).astype(bf16)

    def block_ready(dd):
        for c in range(3):
            arrive(cols.at[dd, pl.ds(IQ * c, IQ)], ring + ND * c + dd)

    @pl.when(image)
    def _():
        emb = r["ei"][...].reshape(IR, WT)
        row = (t * ND + d) * IR + lax.broadcasted_iota(jnp.int32, (IR, TQ), 0) + label[0, 0]
        target = jnp.where(row >= BATCH, row - BATCH, row)
        lane = lax.broadcasted_iota(jnp.int32, (IR, TQ), 1)

        def block(dd):
            pw = weight(dot_t(emb, cols[dd]), target == lane + (dd * TR + m * TQ))
            return dot(pw, cols[dd])

        r["q4t"][0:IR] = block(d)

        def step(k, carry):
            dd = (d + k) % ND
            block_ready(dd)
            r["q4t"][0:IR] += block(dd)
            return carry

        lax.fori_loop(1, ND, step, 0)

    @pl.when(text)
    def _():
        emb = r["et"][...].reshape(TR, WT)
        row = d * TR + lax.broadcasted_iota(jnp.int32, (TR, TQ), 0)
        lane = lax.broadcasted_iota(jnp.int32, (1, TQ), 1)
        part = lane // IQ

        def block(dd):
            off = r["lab"][dd]
            off = jnp.where(part == 0, off[0, :1, :TQ], jnp.where(part == 1, off[1, :1, :TQ], off[2, :1, :TQ]))
            own = (part * ND + dd) * IR + m * IQ + lane % IQ
            target = own + off.astype(jnp.int32)
            target = jnp.where(target >= BATCH, target - BATCH, target)
            pw = weight(dot_t(emb, cols[dd]), row == target)
            return dot(pw, cols[dd])

        r["q4t"][...] = block(d)

        def step(k, carry):
            dd = (d + k) % ND
            block_ready(dd)
            r["q4t"][...] += block(dd)
            return carry

        lax.fori_loop(1, ND, step, 0)

    @pl.when(image)
    def _():
        s4i_start()
        s4i_mid()
        part = s4i_fin()
        grad = part + r["rx4t"][0:IQ].astype(f32)
        length = r["ln"][...]
        direction = r["pr"][...] / length
        pg = ((grad - direction * jnp.sum(direction * grad, axis=1, keepdims=True)) / length).astype(bf16)
        r["bfi"][m] = dot(pg, r["pj"][...]).astype(bf16)
        r["pgf"][...] = pg

    @pl.when(text)
    def _():
        s4t_start()
        s4t_mid()
        part = s4t_fin()
        grad = part + r["rx4t"][...].astype(f32)
        length = r["tl"][...]
        direction = r["tb"][...] / length
        blended_grad = (grad - direction * jnp.sum(direction * grad, axis=1, keepdims=True)) / length
        r["bft"][m] = blended_grad.astype(bf16)

    @pl.when(image)
    def _():
        bi_start()
        for k in range(NM):
            r["pgs"][k] = r["pgf"][:, k * TS:(k + 1) * TS]
        r["pgr"][m] = r["pgs"][m]
        for c in pg_out:
            c.start()
        bl_fin()
        blx_si()
        r["al"][ti] = r["bl"][:, ti]
        r["an"][ti] = r["ns"][pl.ds(pl.multiple_of(ti * IS, IS), IS), :]
        bi_mid()
        bi_fin()
        r["bsi"][...] = r["bfi"][...].reshape(IR, WI).T
        bg_si()
        r["ab"][ti] = r["bsi"][pl.ds(pl.multiple_of(ti * IS, IS), IS), :]

    @pl.when(text)
    def _():
        bt_start()
        r["ant"][...] = r["nt"][(NT - 1) * TS:]
        bt_mid()
        bt_fin()
        r["bst"][...] = r["bft"][...].reshape(TR, WT).T
        bg_st()
        r["abt"][...] = r["bst"][(NT - 1) * TS:]

    @pl.when(image)
    def _():
        for j in range(FI // FC):
            for lo, wide in ((0, 384), (384, 256)):
                at = slice(j * FC + lo, j * FC + lo + wide)
                hg = dot_t(r["bfi"][...].reshape(IR, WI), r["w2"][at, :])
                r["ki"][ti, :, at] = (hg * r["gi"][:, at]).astype(bf16)
            pre[j][0]()
        for dev in (opp, diag, sib):
            arrive(r["pgr"].at[dev[2]], pgb + dev[2])
        pgx_si()
        r["bj"][ti] = r["pgr"][...]

    @pl.when(text)
    def _():
        for at in (slice(0, 384), slice(384, 640)):
            hg = dot_t(r["bft"][...].reshape(TR, WT), r["w2"][at, 0:WT])
            r["kt"][:, at] = (hg * r["gt"][:, at]).astype(bf16)
        pre[0][1]()

    def by_z(g, own, dst, at):
        for p in range(4):
            pair = [g[(q * 4 + p) * own:(q * 4 + p + 1) * own] for q in range(2)]
            dst(p)[:, at] = jnp.concatenate(pair, axis=0).astype(bf16)

    def by_y(g, own, dst, at):
        for p in range(2):
            dst(p)[:, at] = g[p * 4 * own:(p + 1) * 4 * own].astype(bf16)

    def product(lhs, rhs, put, own, dst, begin, width):
        done = 0
        while done < width:
            wide = min(384, width - done)
            put(dot(lhs, rhs(slice(begin + done, begin + done + wide))), own, dst, slice(done, done + wide))
            done += wide

    def three(name):
        return jnp.concatenate([r[name][s] for s in range(3)], axis=1)

    hid_fin()
    bg_fin()
    for j in range(FI // FC):
        product(three("ab"), lambda at: r["hi"][:, :, at].reshape(3 * IR, at.stop - at.start),
                by_z, IO, lambda p, j=j: sb2(j, p), j * FC, FC)
        w2_steps[j][0]()
    product(r["abt"][...], lambda at: r["ht"][:, at], by_y, TO, lambda p: r["sbt2"].at[p], 0, FT)
    t2_steps[0][0]()

    @pl.when(image)
    def _():
        total = jnp.zeros((1, IR), f32)
        for k in range(NM):
            g = dot_t(r["w1"][k * IS:(k + 1) * IS, :], r["ki"][ti])
            total = total + jnp.sum(r["ns"][k * IS:(k + 1) * IS, :].astype(f32) * g, axis=0, keepdims=True)
            r["g6i"][k, 0:IS, :] = g
        tail = jnp.broadcast_to(total, (16, IR))
        for k in range(NM):
            r["g6i"][k, IS:IG, :] = tail
        s6i_start()

    @pl.when(text)
    def _():
        total = jnp.zeros((1, TR), f32)
        for k in range(NM):
            g = dot_t(r["w1"][k * TS:(k + 1) * TS, 0:FT], r["kt"][...])
            total = total + jnp.sum(r["nt"][k * TS:(k + 1) * TS, :].astype(f32) * g, axis=0, keepdims=True)
            r["g6t"][k, 0:TS, :] = g
        tail = jnp.broadcast_to(total, (16, TR))
        for k in range(NM):
            r["g6t"][k, TS:TG, :] = tail
        s6t_start()

    nor_fin()
    for j in range(FI // FC):
        pre[j][2]()
        product(three("an"), lambda at: r["ki"][:, :, at].reshape(3 * IR, at.stop - at.start),
                by_y, IO, lambda p, j=j: sb1(j, p), j * FC, FC)
        w1_steps[j][0]()
        if j == 0:
            @pl.when(image)
            def _():
                s6i_mid()

            @pl.when(text)
            def _():
                s6t_mid()
        w2_steps[j][1]()
    product(r["ant"][...], lambda at: r["kt"][:, at], by_z, TO, lambda p: r["sbt1"].at[p], 0, FT)
    t1_steps[0][0]()
    blx_fin()
    pgx_fin()
    by_y(dot_rows(r["al"][...].reshape(3 * IR, IS), r["bj"][...].reshape(3 * IR, TS)), IO, lambda p: r["sbj"].at[p], slice(0, TS))
    pj_steps[0][0]()

    @pl.when(image)
    def _():
        part = s6i_fin()
        other = r["rx6i"][...].astype(f32)
        average = (part[IS:IS + 1] + other[IS:IS + 1] + other[IS + 1:IS + 2]) / WI
        grad = part[:IS] + other[:IS]
        inv = r["ivi"][...]
        normed = r["xs"][mi, :].astype(f32) * inv
        o_img[0] = r["bsi"][mi, :].astype(f32) + (grad - normed * average) * inv
        o_txt[0] = jnp.zeros((TS, TR), f32)

    @pl.when(text)
    def _():
        part = s6t_fin()
        other = r["rx6t"][...].astype(f32)
        average = (part[TS:TS + 1] + other[TS:TS + 1] + other[TS + 1:TS + 2]) / WT
        grad = part[:TS] + other[:TS]
        inv = r["ivt"][...]
        normed = r["xt"][mt, :].astype(f32) * inv
        o_txt[0] = r["bst"][mt, :].astype(f32) + (grad - normed * average) * inv
        o_img[0] = jnp.zeros((IS, IR), f32)

    t2_steps[0][1]()
    for j in range(FI // FC):
        w1_steps[j][1]()
    t1_steps[0][1]()
    pj_steps[0][1]()
    for j in range(FI // FC):
        w2_steps[j][2](o_w2)
    t2_steps[0][2](o_t2)
    for j in range(FI // FC):
        w1_steps[j][2](o_w1)
    t1_steps[0][2](o_t1)
    pj_steps[0][2](o_pj)

    for c in all_sends:
        c.wait_send()

    @pl.when(image)
    def _():
        for c in img_sends:
            c.wait_send()

    @pl.when(text)
    def _():
        for c in txt_sends:
            c.wait_send()


def move(*refs):
    n = len(refs) // 2
    sem = refs[-1]
    copies = [pltpu.make_async_copy(refs[k], refs[n + k], sem.at[k]) for k in range(n)]
    for c in copies:
        c.start()
    for c in copies:
        c.wait()


def per_device(
    image_in, text_in, img_w1, img_w2, img_proj, txt_w1, txt_w2, label_offset,
    logit_scale, logit_bias, loss_scale,
):
    anywhere = pl.BlockSpec(memory_space=pl.ANY)
    scalar = pl.BlockSpec(memory_space=pltpu.SMEM)
    vmem = pl.BlockSpec(memory_space=pltpu.VMEM)
    one = lambda v: v.reshape(1, 1)
    outs = pl.pallas_call(
        step_kernel,
        out_shape=[
            jax.ShapeDtypeStruct((1, IS, IR), f32),
            jax.ShapeDtypeStruct((1, TS, TR), f32),
            jax.ShapeDtypeStruct((IO, FI), f32),
            jax.ShapeDtypeStruct((IO, FI), f32),
            jax.ShapeDtypeStruct((IO, TS), f32),
            jax.ShapeDtypeStruct((TO, FT), f32),
            jax.ShapeDtypeStruct((TO, FT), f32),
        ],
        in_specs=[anywhere] * 7 + [scalar] * 4,
        out_specs=[vmem] * 7,
        scratch_shapes=list(scratch_list().values()),
        compiler_params=pltpu.CompilerParams(
            collective_id=0, has_side_effects=True, vmem_limit_bytes=63 << 20
        ),
        name="step",
    )(
        image_in.swapaxes(1, 2), text_in.swapaxes(1, 2), img_w1, img_w2, img_proj.T, txt_w1, txt_w2, label_offset,
        one(logit_scale), one(logit_bias), one(loss_scale),
    )
    outs = pl.pallas_call(
        move,
        out_shape=[jax.ShapeDtypeStruct(o.shape, o.dtype) for o in outs],
        in_specs=[anywhere] * len(outs),
        out_specs=[vmem] * len(outs),
        scratch_shapes=[pltpu.SemaphoreType.DMA((len(outs),))],
        name="place",
    )(*outs)
    g_img, g_txt, g_w1, g_w2, g_pj, g_t1, g_t2 = outs
    return (g_img.swapaxes(1, 2), g_txt.swapaxes(1, 2), g_w1, g_w2.T, g_pj, g_t1, g_t2.T)


def solution(mesh):
    return jax.shard_map(
        per_device,
        mesh=mesh,
        in_specs=(
            P("tower", "dp", "mp"),
            P("tower", "dp", "mp"),
            P(None, "mp"),
            P("mp", None),
            P(None, "mp"),
            P(None, "mp"),
            P("mp", None),
            P("tower", "dp"),
            P(),
            P(),
            P(),
        ),
        out_specs=(
            P("tower", "dp", "mp"),
            P("tower", "dp", "mp"),
            P(("tower", "dp"), "mp"),
            P("mp", ("tower", "dp")),
            P(("tower", "dp"), "mp"),
            P(("tower", "dp"), "mp"),
            P("mp", ("tower", "dp")),
        ),
        check_vma=False,
    )
```

time: 210 us -> 170 us (0.81); the launches traced: 207 us -> 170 us
  Pallas kernels: 191 us -> 166 us
  local copies, waits for them, and re-layouts: 13.3 us -> 0 us
    pallas_call x1 -> x2, Pallas kernels: 191 us -> 166 us  [the longest x1 164 us: per_device(): pl.pallas_call(step_kernel, out_shape=[jax.ShapeDtypeStruct((1, IS, IR),...]
    unnamed x20 -> x0, local copies, waits for them, and re-layouts: 13.3 us -> none
where the time goes in v2:
time: 170 us
  Pallas kernels  166 us (98%)
  between operations  3.39 us (2%)
    pallas_call x1, Pallas kernels, per_device(): pl.pallas_call(step_kernel, out_shape=[jax.ShapeDtypeStruct((1, IS, IR),...  164 us

profile of v2, /device:TPU:12, one launch (start us, length us, event | category | flops | bytes accessed | tf_op | source)
XLA Modules:
  0.0 169.9 jit_solution(8760606598969643124)
XLA Ops:
  3.2 163.7 %step.1 = (f32[1,448,128]{2,1,0:T(8,128)}, f32[1,288,384]{2,1,0:T(8,128)}, f32[56,1920]{1,0:T(8,128)}, f32[56,1920]{1,0:T(8,128)}, f32[56,288]{1,0:T(8,128)}, /*index=5*/f32[36,640]{1,0:T(8,128)}, f32[36,640]{1,0:T(8,128)}) custom-call(bf16[1,448,128]{2,1,0:T(8,128)(2,1)} %bitcast.15, bf16[1,288,384]{2,1,0:T(8,128)(2,1)} %bitcast.14, ...), custom_call_target="tpu_custom_call" | custom-call | tf_op jit(solution)/shard_map/step/pallas_call | solution.py:859
  167.0 2.7 %place.1 = (f32[1,448,128]{2,1,0:T(8,128)}, f32[1,288,384]{2,1,0:T(8,128)}, f32[56,1920]{1,0:T(8,128)}, f32[56,1920]{1,0:T(8,128)}, f32[56,288]{1,0:T(8,128)}, /*index=5*/f32[36,640]{1,0:T(8,128)}, f32[36,640]{1,0:T(8,128)}) custom-call(f32[1,448,128]{2,1,0:T(8,128)} %get-tuple-element.21.refs_0_, f32[1,288,384]{2,1,0:T(8,128)} %get-tuple-element.22.refs_1_, ...), custom_call_target="tpu_custom_call" | custom-call | tf_op jit(solution)/shard_map/place/pallas_call | solution.py:881

commit v3 on v2

--- a/solution.py
+++ b/solution.py
@@ -171,6 +171,7 @@
     sib, opp, diag = (t, d, ms), (t, d, mo), (t, d, md)
     dy = d // 4
     dz = d % 4
+    flip = (t, (d + 4) % ND, mo)
     others_t = [((t + k) % NT, d, m) for k in (1, 2, 3)]
     order_d = (4, 1, 3, 5, 7, 2, 6)
     others_d = [(d + k) % ND for k in order_d]
@@ -350,7 +351,40 @@
 
     xi_start, xi_mid, xi_fin = gather_mp(lambda i: r["xs"].at[pl.ds(pl.multiple_of(i * IS, IS), IS)], img_sends)
     xt_start, xt_mid, xt_fin = gather_mp(lambda i: r["xt"].at[pl.ds(pl.multiple_of(i * TS, TS), TS)], txt_sends)
-    pj_start, pj_mid, pj_fin = gather_mp(lambda i: r["pj"].at[pl.ds(pl.multiple_of(i * TS, TS), TS)], img_sends)
+    def head_piece(i, z):
+        row = pl.multiple_of(i * TS + (z // 2) * (TS // 2), TS // 2)
+        lane = pl.multiple_of((z % 2) * (WI // 2), WI // 2)
+        return r["pj"].at[pl.ds(row, TS // 2), pl.ds(lane, WI // 2)]
+
+    def head_slice(i):
+        return r["pj"].at[pl.ds(pl.multiple_of(i * TS, TS), TS)]
+
+    other_z = [(dz + k) % 4 for k in (1, 3, 2)]
+    pjb, pjs, pjz = take(1), take(5), take(4)
+    pj_cross = send(head_piece(m, dz), head_piece(m, dz), pjb, flip, img_sends)
+    pj_own = send(head_slice(m), head_slice(m), pjs + 4, sib, img_sends)
+    pj_spread = [send(head_piece(mo, dz), head_piece(mo, dz), pjz + dz, (t, dy * 4 + z, m), img_sends) for z in other_z]
+    pj_pass = [send(head_piece(mo, z), head_piece(mo, z), pjs + z, sib, img_sends) for z in [dz] + other_z]
+
+    def pj_start():
+        pj_cross.start()
+        pj_own.start()
+
+    def pj_mid():
+        arrive(head_piece(mo, dz), pjb)
+        for c in pj_spread:
+            c.start()
+        pj_pass[0].start()
+
+    def pj_fin():
+        for z, c in zip(other_z, pj_pass[1:]):
+            arrive(head_piece(mo, z), pjz + z)
+            c.start()
+        arrive(head_slice(ms), pjs + 4)
+        for z in range(4):
+            arrive(head_piece(md, z), pjs + z)
+
+    pj_start, pj_mid, pj_fin = plan(img_sends, pj_start, pj_mid, pj_fin)
 
     lab_b = take(3)
     lab_up = send(r["labo"], r["lab"].at[d, ti], lab_b + ti, (NT - 1, d, m), img_sends)
@@ -376,8 +410,12 @@
     ei_start, ei_mid, ei_fin = gather_mp(lambda i: r["ei"].at[i], img_sends)
     et_start, et_mid, et_fin = gather_mp(lambda i: r["et"].at[i], txt_sends)
     bl_start, bl_mid, bl_fin = gather_mp(lambda i: r["bl"].at[i], img_sends)
-    hid_si, hid_st, hid_fin = exchange_x(
-        lambda s: r["hi"].at[ti], lambda s: r["hi"].at[s], lambda s: r["ht"], r["ht"])
+    hid = []
+    for j in range(FI // FC):
+        at = slice(j * FC, (j + 1) * FC)
+        hid.append(exchange_x(
+            lambda s, at=at: r["hi"].at[ti, :, at], lambda s, at=at: r["hi"].at[s, :, at],
+            (lambda s: r["ht"]) if j == 0 else None, r["ht"]))
     nor_si, nor_st, nor_fin = exchange_x(
         lambda s: r["ns"].at[pl.ds(s * IS, IS)], lambda s: r["an"].at[s], lambda s: r["nt"].at[pl.ds(s * TS, TS)], r["ant"])
     blx_si, _, blx_fin = exchange_x(
@@ -442,7 +480,7 @@
         load_t2.start()
 
     barrier = pltpu.get_barrier_semaphore()
-    partners = [sib, opp, diag] + others_t + [(t, dd, m) for dd in others_d]
+    partners = [sib, opp, diag, flip] + others_t + [(t, dd, m) for dd in others_d]
     for dev in partners:
         pl.semaphore_signal(barrier, inc=1, device_id=dev, device_id_type=MESH)
     pl.semaphore_wait(barrier, len(partners))
@@ -461,6 +499,7 @@
         inv = lax.rsqrt(jnp.sum(xt32 * xt32, axis=0, keepdims=True) / WI + epsilon)
         r["ivi"][...] = inv
         r["ns"][...] = (xt32 * inv).astype(bf16)
+        nor_si()
         r["nf"][...] = r["ns"][...].T
 
     @pl.when(text)
@@ -473,6 +512,7 @@
         inv = lax.rsqrt(jnp.sum(xt32 * xt32, axis=0, keepdims=True) / WT + epsilon)
         r["ivt"][...] = inv
         r["nt"][...] = (xt32 * inv).astype(bf16)
+        nor_st()
         r["ntf"][...] = r["nt"][...].T
 
     @pl.when(image)
@@ -500,6 +540,8 @@
 
     @pl.when(image)
     def _():
+        hid[0][0]()
+        hid[1][0]()
         load_w2.wait()
 
         def back(j, carry):
@@ -526,8 +568,9 @@
 
     @pl.when(image)
     def _():
+        s2i_start()
+        pj_mid()
         r["xf"][...] = r["xs"][...].T
-        s2i_start()
         s2i_mid()
         part = s2i_fin()
         rows = pl.ds(pl.multiple_of(m * IQ, IQ), IQ)
@@ -535,7 +578,6 @@
         blended = (x + (part + r["rx2i"][...].astype(f32))).astype(bf16)
         for k in range(NM):
             r["bl"][m, k] = blended[:, k * IS:(k + 1) * IS]
-        pj_mid()
         pj_fin()
         projected = dot_t(blended, r["pj"][...])
         length = jnp.sqrt(jnp.sum(projected * projected, axis=1, keepdims=True))
@@ -548,8 +590,8 @@
 
     @pl.when(text)
     def _():
+        s2t_start()
         r["xtf"][...] = r["xt"][...].T
-        s2t_start()
         s2t_mid()
         part = s2t_fin()
         rows = pl.ds(pl.multiple_of(m * TQ, TQ), TQ)
@@ -571,16 +613,14 @@
     @pl.when(image)
     def _():
         ei_mid()
-        hid_si()
-        nor_si()
+        hid[2][0]()
         bl_mid()
         ei_fin()
 
     @pl.when(text)
     def _():
         et_mid()
-        hid_st()
-        nor_st()
+        hid[0][1]()
         et_fin()
         for dd in others_d:
             arrive(r["lab"].at[dd], lab_d + dd)
@@ -734,9 +774,9 @@
     def three(name):
         return jnp.concatenate([r[name][s] for s in range(3)], axis=1)
 
-    hid_fin()
     bg_fin()
     for j in range(FI // FC):
+        hid[j][2]()
         product(three("ab"), lambda at: r["hi"][:, :, at].reshape(3 * IR, at.stop - at.start),
                 by_z, IO, lambda p, j=j: sb2(j, p), j * FC, FC)
         w2_steps[j][0]()

time: 170 us -> 164 us (0.965)
  Pallas kernels: 166 us -> 160 us
    pallas_call x1, Pallas kernels: 164 us -> 158 us  [per_device(): pl.pallas_call(step_kernel, out_shape=[jax.ShapeDtypeStruct((1, IS, IR),...]
where the time goes in v3:
time: 164 us
  Pallas kernels  160 us (98%)
  between operations  3.39 us (2%)
    pallas_call x1, Pallas kernels, per_device(): pl.pallas_call(step_kernel, out_shape=[jax.ShapeDtypeStruct((1, IS, IR),...  158 us

profile of v3, /device:TPU:12, one launch (start us, length us, event | category | flops | bytes accessed | tf_op | source)
XLA Modules:
  0.0 163.8 jit_solution(14422126832176863101)
XLA Ops:
  3.2 157.6 %step.1 = (f32[1,448,128]{2,1,0:T(8,128)}, f32[1,288,384]{2,1,0:T(8,128)}, f32[56,1920]{1,0:T(8,128)}, f32[56,1920]{1,0:T(8,128)}, f32[56,288]{1,0:T(8,128)}, /*index=5*/f32[36,640]{1,0:T(8,128)}, f32[36,640]{1,0:T(8,128)}) custom-call(bf16[1,448,128]{2,1,0:T(8,128)(2,1)} %bitcast.15, bf16[1,288,384]{2,1,0:T(8,128)(2,1)} %bitcast.14, ...), custom_call_target="tpu_custom_call" | custom-call | tf_op jit(solution)/shard_map/step/pallas_call | solution.py:899
  160.9 2.7 %place.1 = (f32[1,448,128]{2,1,0:T(8,128)}, f32[1,288,384]{2,1,0:T(8,128)}, f32[56,1920]{1,0:T(8,128)}, f32[56,1920]{1,0:T(8,128)}, f32[56,288]{1,0:T(8,128)}, /*index=5*/f32[36,640]{1,0:T(8,128)}, f32[36,640]{1,0:T(8,128)}) custom-call(f32[1,448,128]{2,1,0:T(8,128)} %get-tuple-element.21.refs_0_, f32[1,288,384]{2,1,0:T(8,128)} %get-tuple-element.22.refs_1_, ...), custom_call_target="tpu_custom_call" | custom-call | tf_op jit(solution)/shard_map/place/pallas_call | solution.py:921

commit v4 on v3

--- a/solution.py
+++ b/solution.py
@@ -125,9 +125,9 @@
         st6t=v((TG, TR), bf16),
         rx6i=v((IG, IR), bf16),
         rx6t=v((TG, TR), bf16),
-        ra1=v((2, 4 * IO, FI), bf16),
-        sc1=v((4, IP, FI), bf16),
-        rc1=v((4, IP, FI), bf16),
+        ra1=v((2, 4 * IO, 2 * FC), bf16),
+        sc1=v((4, IP, 2 * FC), bf16),
+        rc1=v((4, IP, 2 * FC), bf16),
         ra2=v((4, 2 * IO, FI), bf16),
         sc2=v((2, IP, FI), bf16),
         rc2=v((2, IP, FI), bf16),
@@ -139,10 +139,13 @@
         rat1=v((4, 2 * TO, FT), bf16),
         sct1=v((2, TP, FT), bf16),
         rct1=v((2, TP, FT), bf16),
-        sbt2=v((2, 4 * TO, FT), bf16),
-        rat2=v((2, 4 * TO, FT), bf16),
-        sct2=v((4, TP, FT), bf16),
-        rct2=v((4, TP, FT), bf16),
+        sbt2=v((4, 2 * TO, FT), bf16),
+        rat2=v((4, 2 * TO, FT), bf16),
+        sct2=v((2, TP, FT), bf16),
+        rct2=v((2, TP, FT), bf16),
+        ra1z=v((4, 2 * IO, FC), bf16),
+        sc1z=v((2, IP, FC), bf16),
+        rc1z=v((2, IP, FC), bf16),
         sem=pltpu.SemaphoreType.DMA((N_SEM,)),
     )
 
@@ -325,13 +328,13 @@
                 for c in c2:
                     c.start()
 
-            def finish(out=None, span=span, two=two, b2=b2):
+            def finish(out=None, at=None, span=span, two=two, b2=b2):
                 total = second[rest, :, span].astype(f32)
                 for p in two:
                     arrive(second_in.at[p, :, span], b2 + p)
                     total = total + second_in[p, :, span].astype(f32)
                 if out is not None:
-                    out[:, span] = total[:own]
+                    out[:, at or span] = total[:own]
 
             steps.append(plan(all_sends, start, middle, finish))
         return steps
@@ -458,11 +461,15 @@
     def sb1(j, p):
         return r["w1"].at[pl.ds(pl.multiple_of(p * 4 * IO, 4 * IO), 4 * IO), spans[j]]
 
+    def sb1z(p):
+        return r["w1"].at[pl.ds(pl.multiple_of(p * 2 * IO, 2 * IO), 2 * IO), spans[2]]
+
     w2_steps = scatter_dp(
         "z", IO, IP, spans, sb2, r["ra2"], r["sc2"], r["rc2"])
     w1_steps = scatter_dp(
-        "y", IO, IP, spans, sb1, r["ra1"], r["sc1"], r["rc1"])
-    t2_steps = scatter_dp("y", TO, TP, whole_t, lambda j, p: r["sbt2"].at[p], r["rat2"], r["sct2"], r["rct2"])
+        "y", IO, IP, spans[:2], sb1, r["ra1"], r["sc1"], r["rc1"])
+    w1_steps += scatter_dp("z", IO, IP, [slice(0, FC)], lambda j, p: sb1z(p), r["ra1z"], r["sc1z"], r["rc1z"])
+    t2_steps = scatter_dp("z", TO, TP, whole_t, lambda j, p: r["sbt2"].at[p], r["rat2"], r["sct2"], r["rct2"])
     t1_steps = scatter_dp("z", TO, TP, whole_t, lambda j, p: r["sbt1"].at[p], r["rat1"], r["sct1"], r["rct1"])
     pj_steps = scatter_dp("y", IO, IP, whole_j, lambda j, p: r["sbj"].at[p], r["raj"], r["scj"], r["rcj"])
 
@@ -742,7 +749,8 @@
                 at = slice(j * FC + lo, j * FC + lo + wide)
                 hg = dot_t(r["bfi"][...].reshape(IR, WI), r["w2"][at, :])
                 r["ki"][ti, :, at] = (hg * r["gi"][:, at]).astype(bf16)
-            pre[j][0]()
+            if j == 0:
+                pre[0][0]()
         for dev in (opp, diag, sib):
             arrive(r["pgr"].at[dev[2]], pgb + dev[2])
         pgx_si()
@@ -780,7 +788,11 @@
         product(three("ab"), lambda at: r["hi"][:, :, at].reshape(3 * IR, at.stop - at.start),
                 by_z, IO, lambda p, j=j: sb2(j, p), j * FC, FC)
         w2_steps[j][0]()
-    product(r["abt"][...], lambda at: r["ht"][:, at], by_y, TO, lambda p: r["sbt2"].at[p], 0, FT)
+        if j == 1:
+            @pl.when(image)
+            def _():
+                pre[1][0]()
+    product(r["abt"][...], lambda at: r["ht"][:, at], by_z, TO, lambda p: r["sbt2"].at[p], 0, FT)
     t2_steps[0][0]()
 
     @pl.when(image)
@@ -794,6 +806,7 @@
         for k in range(NM):
             r["g6i"][k, IS:IG, :] = tail
         s6i_start()
+        pre[2][0]()
 
     @pl.when(text)
     def _():
@@ -807,11 +820,16 @@
             r["g6t"][k, TS:TG, :] = tail
         s6t_start()
 
+    blx_fin()
+    pgx_fin()
+    by_y(dot_rows(r["al"][...].reshape(3 * IR, IS), r["bj"][...].reshape(3 * IR, TS)), IO,
+         lambda p: r["sbj"].at[p], slice(0, TS))
+    pj_steps[0][0]()
     nor_fin()
     for j in range(FI // FC):
         pre[j][2]()
         product(three("an"), lambda at: r["ki"][:, :, at].reshape(3 * IR, at.stop - at.start),
-                by_y, IO, lambda p, j=j: sb1(j, p), j * FC, FC)
+                by_z if j == 2 else by_y, IO, (lambda p: sb1z(p)) if j == 2 else (lambda p, j=j: sb1(j, p)), j * FC, FC)
         w1_steps[j][0]()
         if j == 0:
             @pl.when(image)
@@ -821,13 +839,14 @@
             @pl.when(text)
             def _():
                 s6t_mid()
+            product(r["ant"][...], lambda at: r["kt"][:, at], by_z, TO, lambda p: r["sbt1"].at[p], 0, FT)
+            t1_steps[0][0]()
         w2_steps[j][1]()
-    product(r["ant"][...], lambda at: r["kt"][:, at], by_z, TO, lambda p: r["sbt1"].at[p], 0, FT)
-    t1_steps[0][0]()
-    blx_fin()
-    pgx_fin()
-    by_y(dot_rows(r["al"][...].reshape(3 * IR, IS), r["bj"][...].reshape(3 * IR, TS)), IO, lambda p: r["sbj"].at[p], slice(0, TS))
-    pj_steps[0][0]()
+        if j == 1:
+            t2_steps[0][1]()
+            w1_steps[0][1]()
+    w1_steps[1][1]()
+    pj_steps[0][1]()
 
     @pl.when(image)
     def _():
@@ -851,18 +870,15 @@
         o_txt[0] = r["bst"][mt, :].astype(f32) + (grad - normed * average) * inv
         o_img[0] = jnp.zeros((IS, IR), f32)
 
-    t2_steps[0][1]()
-    for j in range(FI // FC):
-        w1_steps[j][1]()
+    w1_steps[2][1]()
     t1_steps[0][1]()
-    pj_steps[0][1]()
     for j in range(FI // FC):
         w2_steps[j][2](o_w2)
     t2_steps[0][2](o_t2)
+    pj_steps[0][2](o_pj)
     for j in range(FI // FC):
-        w1_steps[j][2](o_w1)
+        w1_steps[j][2](o_w1, spans[j])
     t1_steps[0][2](o_t1)
-    pj_steps[0][2](o_pj)
 
     for c in all_sends:
         c.wait_send()

time: 164 us -> 153 us (0.933)
  Pallas kernels: 160 us -> 150 us
    pallas_call x1, Pallas kernels: 158 us -> 147 us  [per_device(): pl.pallas_call(step_kernel, out_shape=[jax.ShapeDtypeStruct((1, IS, IR),...]
where the time goes in v4:
time: 153 us
  Pallas kernels  150 us (98%)
  between operations  3.39 us (2%)
    pallas_call x1, Pallas kernels, per_device(): pl.pallas_call(step_kernel, out_shape=[jax.ShapeDtypeStruct((1, IS, IR),...  147 us

profile of v4, /device:TPU:12, one launch (start us, length us, event | category | flops | bytes accessed | tf_op | source)
XLA Modules:
  0.0 153.3 jit_solution(10095341765098960657)
XLA Ops:
  3.2 147.2 %step.1 = (f32[1,448,128]{2,1,0:T(8,128)}, f32[1,288,384]{2,1,0:T(8,128)}, f32[56,1920]{1,0:T(8,128)}, f32[56,1920]{1,0:T(8,128)}, f32[56,288]{1,0:T(8,128)}, /*index=5*/f32[36,640]{1,0:T(8,128)}, f32[36,640]{1,0:T(8,128)}) custom-call(bf16[1,448,128]{2,1,0:T(8,128)(2,1)} %bitcast.15, bf16[1,288,384]{2,1,0:T(8,128)(2,1)} %bitcast.14, ...), custom_call_target="tpu_custom_call" | custom-call | tf_op jit(solution)/shard_map/step/pallas_call | solution.py:915
  150.4 2.7 %place.1 = (f32[1,448,128]{2,1,0:T(8,128)}, f32[1,288,384]{2,1,0:T(8,128)}, f32[56,1920]{1,0:T(8,128)}, f32[56,1920]{1,0:T(8,128)}, f32[56,288]{1,0:T(8,128)}, /*index=5*/f32[36,640]{1,0:T(8,128)}, f32[36,640]{1,0:T(8,128)}) custom-call(f32[1,448,128]{2,1,0:T(8,128)} %get-tuple-element.21.refs_0_, f32[1,288,384]{2,1,0:T(8,128)} %get-tuple-element.22.refs_1_, ...), custom_call_target="tpu_custom_call" | custom-call | tf_op jit(solution)/shard_map/place/pallas_call | solution.py:937

commit v5 on v4

--- a/solution.py
+++ b/solution.py
@@ -792,6 +792,11 @@
             @pl.when(image)
             def _():
                 pre[1][0]()
+    blx_fin()
+    pgx_fin()
+    by_y(dot_rows(r["al"][...].reshape(3 * IR, IS), r["bj"][...].reshape(3 * IR, TS)), IO,
+         lambda p: r["sbj"].at[p], slice(0, TS))
+    pj_steps[0][0]()
     product(r["abt"][...], lambda at: r["ht"][:, at], by_z, TO, lambda p: r["sbt2"].at[p], 0, FT)
     t2_steps[0][0]()
 
@@ -820,11 +825,6 @@
             r["g6t"][k, TS:TG, :] = tail
         s6t_start()
 
-    blx_fin()
-    pgx_fin()
-    by_y(dot_rows(r["al"][...].reshape(3 * IR, IS), r["bj"][...].reshape(3 * IR, TS)), IO,
-         lambda p: r["sbj"].at[p], slice(0, TS))
-    pj_steps[0][0]()
     nor_fin()
     for j in range(FI // FC):
         pre[j][2]()

time: 153 us -> 154 us (level)
  no operation moved by 1% of the time
where the time goes in v5:
time: 154 us; the launch traced here: 153 us
  Pallas kernels  150 us (97%)
  between operations  3.39 us (2%)
    pallas_call x1, Pallas kernels, per_device(): pl.pallas_call(step_kernel, out_shape=[jax.ShapeDtypeStruct((1, IS, IR),...  147 us

profile of v5, /device:TPU:12, one launch (start us, length us, event | category | flops | bytes accessed | tf_op | source)
XLA Modules:
  0.0 153.4 jit_solution(3960379262116011832)
XLA Ops:
  3.2 147.3 %step.1 = (f32[1,448,128]{2,1,0:T(8,128)}, f32[1,288,384]{2,1,0:T(8,128)}, f32[56,1920]{1,0:T(8,128)}, f32[56,1920]{1,0:T(8,128)}, f32[56,288]{1,0:T(8,128)}, /*index=5*/f32[36,640]{1,0:T(8,128)}, f32[36,640]{1,0:T(8,128)}) custom-call(bf16[1,448,128]{2,1,0:T(8,128)(2,1)} %bitcast.15, bf16[1,288,384]{2,1,0:T(8,128)(2,1)} %bitcast.14, ...), custom_call_target="tpu_custom_call" | custom-call | tf_op jit(solution)/shard_map/step/pallas_call | solution.py:915
  150.5 2.7 %place.1 = (f32[1,448,128]{2,1,0:T(8,128)}, f32[1,288,384]{2,1,0:T(8,128)}, f32[56,1920]{1,0:T(8,128)}, f32[56,1920]{1,0:T(8,128)}, f32[56,288]{1,0:T(8,128)}, /*index=5*/f32[36,640]{1,0:T(8,128)}, f32[36,640]{1,0:T(8,128)}) custom-call(f32[1,448,128]{2,1,0:T(8,128)} %get-tuple-element.21.refs_0_, f32[1,288,384]{2,1,0:T(8,128)} %get-tuple-element.22.refs_1_, ...), custom_call_target="tpu_custom_call" | custom-call | tf_op jit(solution)/shard_map/place/pallas_call | solution.py:937
